TPU v7x, 128 devices: a whole 4x4x4 slice. The times are simulated.
128 devices in a mesh: ctx: 32 (over x_hi, z, y), ch: 4 (over x_lo, core).
Axes of the slice: x: 4 (x_hi: 2, x_lo: 2; x = x_hi * 2 + x_lo), y: 4, z: 4, core: 2. Of those that a mesh axis runs over, the one named last changes fastest.
Arguments:
- prefix_values: bfloat16 [16384, 4096], P('ctx', 'ch'), may hold values from -6 to 6
- suffix_values: bfloat16 [32768, 4096], P('ctx', 'ch'), may hold values from -6 to 6
- suffix_gates: bfloat16 [32768, 4096], P('ctx', 'ch'), may hold values from -6 to 6
- rates: float32 [16, 4096], P(None, 'ch'), may hold values from 4.06901042e-06 to 0.041666667
- residues: float32 [16, 4096], P(None, 'ch'), may hold values from -1.5 to 1.5
- norm_gain: float32 [4096], P('ch'), may hold values from 0.5 to 1.5
- block_order: int32 [64], replicated, may hold values from 0 to 63, each once
- prefix_blocks: int32 [1], replicated, may hold values from 1 to 32
Outputs:
- mixed: bfloat16 [32768, 4096], P('ctx', 'ch')
Inputs may be any that keep to these rules, and one draw needn't show every extreme that they name: `block_order`: each number once.
All inputs are finite; a program needn't handle non-finite values.
Results may differ from a plain program's by a relative error of at most 0.0085.
Values may be sent and summed in bfloat16 or wider, within the bound.
A program may use at most 192 MiB of HBM per device.

v0:
```python
import math

import jax
import jax.numpy as jnp
from jax import lax
from jax.sharding import PartitionSpec as P

HIGH = lax.Precision.HIGHEST


def prefix_state(piece, start, rates, reverse, sub_len, blk, plen):
    rows, chans = piece.shape
    parts = blk // sub_len
    grouped = piece.reshape(rows // blk, parts, sub_len, chans)
    offsets = jnp.arange(parts, dtype=jnp.int32) * sub_len + sub_len - 1

    def add_block(total, index):
        block = grouped[index].astype(jnp.float32)
        states = jnp.einsum("msc,jsc->jmc", reverse, block, precision=HIGH)
        last = start + index * blk + offsets
        lag = (plen - 1 - last).astype(jnp.float32)
        weight = jnp.exp(-rates[None] * jnp.maximum(lag, 0.0)[:, None, None])
        weight = jnp.where((lag >= 0.0)[:, None, None], weight, jnp.float32(0.0))
        return (total + jnp.sum(weight * states, axis=0), None)

    zeros = jnp.zeros((rates.shape[0], chans), jnp.float32)
    total, _ = lax.scan(add_block, zeros, jnp.arange(rows // blk, dtype=jnp.int32))
    return total


def local(
    prefix_values,
    suffix_values,
    suffix_gates,
    rates,
    residues,
    norm_gain,
    block_order,
    prefix_blocks,
):
    blk = prefix_values.shape[0]
    chans = rates.shape[1]
    sub_len = min(128, blk)
    parts = blk // sub_len
    me = lax.axis_index("ctx")
    plen = prefix_blocks[0] * blk
    steps = jnp.arange(blk, dtype=jnp.float32)
    base = jnp.exp(-rates[:, None, :] * steps[None, :, None])
    reverse = base[:, :sub_len][:, ::-1]
    coef = residues * jnp.sqrt(2.0 * rates)
    local_total = prefix_state(prefix_values, me * blk, rates, reverse, sub_len, blk, plen)
    prefix_total = lax.psum(local_total, "ctx")
    own_ids = lax.dynamic_slice_in_dim(block_order, 2 * me, 2, 0)
    values = suffix_values.astype(jnp.float32)
    shaped = values.reshape(2, parts, sub_len, chans)
    pieces = jnp.einsum("msc,bjsc->bjmc", reverse, shaped, precision=HIGH)
    offsets = (jnp.arange(parts, dtype=jnp.int32) * sub_len + sub_len - 1).astype(jnp.float32)
    inner = jnp.exp(-rates[None] * (blk - 1.0 - offsets)[:, None, None])
    ends = jnp.sum(pieces * inner[None], axis=1)
    gap = own_ids[:, None] - block_order[None, :] - 1
    gap_rows = (jnp.maximum(gap, 0) * blk).astype(jnp.float32)
    weight = jnp.exp(-rates[None, None] * gap_rows[:, :, None, None])
    weight = jnp.where((gap >= 0)[:, :, None, None], weight, jnp.float32(0.0))
    incoming = jnp.sum(weight * lax.all_gather(ends, "ctx", axis=0, tiled=True)[None], axis=1)
    own_rows = (own_ids * blk).astype(jnp.float32)
    incoming = incoming + prefix_total[None] * jnp.exp(-rates[None] * own_rows[:, None, None])
    freq = jnp.arange(2 * blk, dtype=jnp.int32)
    times = jnp.arange(blk, dtype=jnp.int32)
    phase = (freq[:, None] * times[None, :] % (2 * blk)).astype(jnp.float32) * (math.pi / blk)
    forward = jnp.concatenate([jnp.cos(phase), -jnp.sin(phase)], 0)
    inverse = jnp.concatenate([jnp.cos(phase).T, -jnp.sin(phase).T], 1) / (2.0 * blk)
    taps = jnp.einsum("mtc,mc->tc", base, coef, precision=HIGH)
    taps_freq = jnp.dot(forward, taps, precision=HIGH)
    spectrum = jnp.einsum("kt,btc->bkc", forward, values.reshape(2, blk, chans), precision=HIGH)
    half = 2 * blk
    real_x = spectrum[:, :half]
    imag_x = spectrum[:, half:]
    real_h = taps_freq[None, :half]
    imag_h = taps_freq[None, half:]
    product = jnp.concatenate(
        [real_x * real_h - imag_x * imag_h, real_x * imag_h + imag_x * real_h], 1
    )
    near = jnp.einsum("tk,bkc->btc", inverse, product, precision=HIGH)
    far = jnp.einsum(
        "mtc,bmc->btc", base, incoming * (jnp.exp(-rates) * coef)[None], precision=HIGH
    )
    conv = (near + far).reshape(2 * blk, chans)
    gated = suffix_gates.astype(jnp.float32) * conv
    squares = lax.psum(jnp.sum(gated * gated, axis=1), "ch")
    scale = lax.rsqrt(squares / (chans * lax.axis_size("ch")) + 1e-06)
    return (gated * scale[:, None] * norm_gain[None, :]).astype(jnp.bfloat16)


def solution(mesh):
    return jax.shard_map(
        local,
        mesh=mesh,
        in_specs=(
            P("ctx", "ch"),
            P("ctx", "ch"),
            P("ctx", "ch"),
            P(None, "ch"),
            P(None, "ch"),
            P("ch"),
            P(),
            P(),
        ),
        out_specs=P("ctx", "ch"),
        check_vma=False,
    )
```

profile of v0, /device:TPU:1, one launch (start us, length us, event | category | flops | bytes accessed | tf_op | source)
XLA Modules:
  0.0 540.1 jit_solution(10888817740222522452)
XLA Ops:
  6.5 0.0 all-gather.2.cloned.1.call-start
  6.5 0.9 fusion.41
  7.5 0.2 copy.19
  7.7 11.4 %multiply_exponential_fusion = f32[16,512,1024]{1,0,2:T(8,128)} fusion(f32[16,1024]{0,1:T(8,128)S(1)} %copy.19), kind=kLoop, calls=%fused_computation | loop fusion | flops 8388608 | bytes 33619968 | tf_op jit(solution)/shard_map/exp | solution.py:48
  19.0 7.1 %slice.24 = f32[16,128,1024]{1,0,2:T(8,128)} slice(f32[16,512,1024]{1,0,2:T(8,128)} %multiply_exponential_fusion), slice={[0:16], [0:128], [0:1024]} | slice | bytes 16777216 | tf_op jit(solution)/shard_map/slice | solution.py:49
  26.2 13.1 %rev.3 = f32[16,128,1024]{1,0,2:T(8,128)} reverse(f32[16,128,1024]{1,0,2:T(8,128)} %slice.24), dimensions={1} | reverse | bytes 16777216 | tf_op jit(solution)/shard_map/rev | solution.py:49
  39.3 2.0 multiply_exponential_fusion.3
  41.3 4.3 copy.20
  45.6 13.4 %fusion.14 = f32[2,16,1024]{1,0,2:T(2,128)S(1)} fusion(bf16[2,4,128,1024]{2,1,0,3:T(4,128)(2,1)} %copy.20, f32[16,128,1024]{1,0,2:T(8,128)} %rev.3, f32[4,16,1024]{1,0,2:T(4,128)} %multiply_exponential_fusion.3), kind=kOutput, calls=%fused_computation.23 | convolution fusion | flops 201555968 | bytes 10878976 | tf_op jit(solution)/shard_map/msc,bjsc->bjmc/dot_general | solution.py:56
  59.0 1.1 copy.30
  60.1 0.0 all-gather.2.cloned.1.call-update
  60.1 0.4 all-reduce.2.cloned.1.call-start
  61.1 1.7 copy.23
  62.9 0.0 copy-start.5
  62.9 12.2 %fusion.29 = f32[16,1024]{0,1:T(8,128)S(1)} fusion(f32[16,128,1024]{1,0,2:T(8,128)} %rev.3, bf16[4,128,1024]{1,0,2:T(4,128)(2,1)S(1)} %copy.23, f32[4]{0:T(128)S(1)} %convert_maximum_fusion, f32[16,1024]{0,1:T(8,128)S(1)} %copy.19, pred[4]{0:T(512)(128)(4,1)S(1)} %convert_compare_fusion), kind=kOutput, calls=%fused_computation.41 | convolution fusion | flops 100909056 | bytes 9568276 | tf_op jit(solution)/shard_map/while/body/eval_jaxpr/msc,jsc->jmc/dot_general | solution.py:19
  75.1 0.8 copy.31
  75.9 0.0 all-reduce.2.cloned.1.call-update
  75.9 0.0 copy-done.5
  76.0 0.1 multiply_convert_fusion.2
  76.0 0.1 multiply_convert_fusion.1
  76.1 0.1 fusion.42
  76.2 9.2 %sine_negate_fusion.1 = (f32[1024,512]{1,0:T(8,128)}, f32[1024,512]{1,0:T(8,128)}) fusion(), kind=kLoop, calls=%fused_computation.49 | loop fusion | flops 7864320 | bytes 4194304 | tf_op jit(solution)/shard_map/neg | solution.py:70
  85.4 9.2 %sine_negate_fusion = (f32[512,1024]{1,0:T(8,128)}, f32[512,1024]{1,0:T(8,128)}) fusion(), kind=kLoop, calls=%fused_computation.46 | loop fusion | flops 7864320 | bytes 4194304 | tf_op jit(solution)/shard_map/neg | solution.py:71
  94.6 0.3 copy.27
  94.9 0.0 copy-start.2
  94.9 0.0 copy-start.3
  94.9 22.7 %fusion.1 = f32[1024,1,512]{2,1,0:T(1,128)S(1)} fusion(f32[16,1024,1]{0,2,1:T(1,128)S(1)} %copy.27, f32[16,1024]{0,1:T(8,128)S(1)} %copy.19), kind=kOutput, calls=%fused_computation.2 | convolution fusion | flops 109051904 | bytes 2228224 | tf_op jit(solution)/shard_map/mtc,mc->tc/dot_general | solution.py:72
  117.6 0.0 copy-done.2
  117.6 0.0 copy-done.3
  117.6 14.8 %fusion.16 = f32[2048,1024]{1,0:T(8,128)S(1)} fusion(f32[1024,512]{1,0:T(8,128)S(1)} %copy-done.2, f32[1024,512]{1,0:T(8,128)S(1)} %copy-done.3, f32[1024,1,512]{2,1,0:T(1,128)S(1)} %fusion.1), kind=kOutput, calls=%fused_computation.27 | convolution fusion | flops 12885950464 | bytes 14680064 | tf_op jit(solution)/shard_map/dot_general | solution.py:73
  132.5 0.8 fusion.47
  133.3 16.9 %convolution_bitcast_fusion = f32[2,2048,1024]{2,1,0:T(8,128)} fusion(bf16[2,512,1024]{2,1,0:T(8,128)(2,1)} %bitcast.51, f32[1024,512]{1,0:T(8,128)S(1)} %copy-done.2, f32[1024,512]{1,0:T(8,128)S(1)} %copy-done.3), kind=kOutput, calls=%fused_computation.14 | convolution fusion | flops 25770852352 | bytes 23068672 | tf_op jit(solution)/shard_map/kt,btc->bkc/dot_general | solution.py:74
  150.2 11.2 %multiply_subtract_fusion = (f32[2,1024,1024]{2,1,0:T(8,128)}, f32[2,1024,1024]{2,1,0:T(8,128)}) fusion(f32[2,2048,1024]{2,1,0:T(8,128)} %convolution_bitcast_fusion, f32[1024,1024]{1,0:T(8,128)S(1)} %get-tuple-element.32, f32[1024,1024]{1,0:T(8,128)S(1)} %get-tuple-element.23), kind=kLoop, calls=%fused_computation.13 | loop fusion | flops 12582912 | bytes 41943040 | tf_op jit(solution)/shard_map/sub | solution.py:81
  161.4 0.0 all-gather.2.cloned.1.call-done
  161.5 3.7 multiply_reduce_fusion
  165.2 280.7 %all-reduce.2.cloned.1.call-done = f32[16,1024]{1,0:T(8,128)} async-done(((f32[16,1024]{1,0:T(8,128)}), f32[16,1024]{1,0:T(8,128)}) %all-reduce.2.cloned.1.call-update) | async-done | bytes 65552 | tf_op jit(solution)/shard_map/psum | solution.py:52
  445.9 0.9 add_multiply_fusion
  446.8 0.5 copy.25
  447.4 23.4 %fusion = f32[1024,2,512]{2,1,0:T(2,128)} fusion(f32[2,16,1024]{1,0,2:T(2,128)S(1)} %copy.25, f32[16,1024]{0,1:T(8,128)S(1)} %copy.19), kind=kOutput, calls=%fused_computation.1 | convolution fusion | flops 209715200 | bytes 4390912 | tf_op jit(solution)/shard_map/mtc,bmc->btc/dot_general | solution.py:84
  470.8 7.2 %copy.26 = f32[1024,2,512]{0,2,1:T(8,128)} copy(f32[1024,2,512]{2,1,0:T(2,128)} %fusion) | data formatting | bytes 8388608 | tf_op jit(solution)/shard_map/mtc,bmc->btc/dot_general | solution.py:84
  478.0 0.0 copy-start.1
  478.0 32.3 %bitcast_add_fusion = f32[2,512,1024]{2,1,0:T(8,128)S(1)} fusion(f32[1024,2,512]{0,2,1:T(8,128)} %copy.26, f32[512,1024]{1,0:T(8,128)} %get-tuple-element.40, f32[512,1024]{1,0:T(8,128)} %get-tuple-element.41, f32[2,1024,1024]{2,1,0:T(8,128)} %get-tuple-element.22, f32[2,1024,1024]{2,1,0:T(8,128)} %get-tuple-element.21), kind=kOutput, calls=%fused_computation.21 | convolution fusion | flops 25777143808 | bytes 29360128 | tf_op jit(solution)/shard_map/tk,bkc->btc/dot_general | solution.py:83
  510.4 0.0 copy-start
  510.4 1.9 copy-done
  512.3 0.0 copy-done.1
  512.3 0.0 copy-start.4
  512.3 0.6 multiply_reduce_fusion.1
  512.9 15.7 %psum.15 = f32[1024]{0:T(1024)S(1)} all-reduce(f32[1024]{0:T(1024)S(1)} %multiply_reduce_fusion.1), channel_id=1, replica_groups=mesh['ctx'=32,'ch'=4] {'ch'}, use_global_device_ids=true, to_apply=%region_5.6 | all-reduce | flops 1024 | bytes 8192 | tf_op jit(solution)/shard_map/psum | solution.py:89
  528.7 0.0 copy-done.4
  528.7 4.2 multiply_convert_fusion
  (4 shorter events, 0.0 us)
Async XLA Ops:
  6.5 154.9 %all-gather.2.cloned.1.call-start = ((), (), s32[]{:S(2)}) async-start(), calls=%async_computation | async-start | bytes 4325376 | tf_op jit(solution)/shard_map/all_gather | solution.py:64
  60.1 385.8 %all-reduce.2.cloned.1.call-start = ((), (), s32[]{:S(2)}) async-start(), calls=%async_computation.1 | async-start | bytes 131072 | tf_op jit(solution)/shard_map/psum | solution.py:52
  62.9 13.0 %copy-start.5 = (s32[64]{0:T(128)S(1)}, s32[64]{0:T(128)}, u32[]{:S(2)}) copy-start(s32[64]{0:T(128)} %param.14) | copy-start | bytes 772
  94.9 22.8 %copy-start.2 = (f32[1024,512]{1,0:T(8,128)S(1)}, f32[1024,512]{1,0:T(8,128)}, u32[]{:S(2)}) copy-start(f32[1024,512]{1,0:T(8,128)} %get-tuple-element.38) | copy-start | bytes 6291460
  94.9 22.8 %copy-start.3 = (f32[1024,512]{1,0:T(8,128)S(1)}, f32[1024,512]{1,0:T(8,128)}, u32[]{:S(2)}) copy-start(f32[1024,512]{1,0:T(8,128)} %get-tuple-element.39) | copy-start | bytes 6291460
  478.0 34.3 %copy-start.1 = (bf16[1024,1024]{1,0:T(8,128)(2,1)S(1)}, bf16[1024,1024]{1,0:T(8,128)(2,1)}, u32[]{:S(2)}) copy-start(bf16[1024,1024]{1,0:T(8,128)(2,1)} %param.10) | copy-start | bytes 6291460
  510.4 1.9 copy-start
  512.3 16.4 %copy-start.4 = (f32[1024]{0:T(1024)S(1)}, f32[1024]{0:T(1024)}, u32[]{:S(2)}) copy-start(f32[1024]{0:T(1024)} %param.13) | copy-start | bytes 12292
Sparse Core Ops, SparseCore 0:
  60.2 83.2 all-gather.1
  146.0 299.8 all-reduce.1
where the time goes:
time: 549 us; the launch traced here: 540 us
  waiting for transfers between devices  281 us (51%)
  matrix products  136 us (25%)
  other arithmetic  53.6 us (10%)
  local copies, waits for them, and re-layouts  39.2 us (7%)
  blocking collectives  15.7 us (3%)
  between operations  14.7 us (3%)
    psum x1, waiting for transfers between devices, local(): prefix_total = lax.psum(local_total, 'ctx')  281 us
    dot_general x1, matrix products, local(): near = jnp.einsum('tk,bkc->btc', inverse, product, precision=HIGH)  32.3 us
    dot_general x1, matrix products, local(): jnp.einsum('mtc,bmc->btc', base, incoming * (jnp.exp(-rates) * coef)[None...  23.4 us
    dot_general x1, matrix products, local(): taps = jnp.einsum('mtc,mc->tc', base, coef, precision=HIGH)  22.7 us
    dot_general x1, matrix products, local(): jnp.einsum('kt,btc->bkc', forward, values.reshape(2, blk, chans), precisi...  16.9 us
    psum x1, blocking collectives, local(): squares = lax.psum(jnp.sum(gated * gated, axis=1), 'ch')  15.7 us
    dot_general x1, matrix products, local(): taps_freq = jnp.dot(forward, taps, precision=HIGH)  14.8 us
    dot_general x1, matrix products, local(): pieces = jnp.einsum('msc,bjsc->bjmc', reverse, shaped, precision=HIGH)  13.4 us
  transfers between devices with their start and end apart: 2, of which 1 were waited for; matrix products, arithmetic and copies ran while one was open for 19% of the time, Pallas kernels for 0%

commit v1 on v0

v1 whole, which is shorter than its diff:
```python
import functools

import jax
import jax.numpy as jnp
import ml_dtypes
import numpy as np
from jax import lax
from jax.experimental import pallas as pl
from jax.experimental.pallas import tpu as pltpu
from jax.sharding import PartitionSpec as P

MESH = pl.DeviceIdType.MESH
F32 = jnp.float32
BF16 = jnp.bfloat16

LEN = 256
ORD = 16
MODES = 16
CTX = 32
CH = 4
CHANS = 1024
TILES = CHANS // 128
RATE_HALF = 1.0 / 48.0
EPS = 1e-6


def series():
    nodes = 64
    angle = np.pi * (np.arange(nodes) + 0.5) / nodes
    rate = RATE_HALF * (1.0 + np.cos(angle))
    values = np.exp(-rate[:, None] * np.arange(LEN)[None, :])
    basis = np.cos(np.arange(ORD)[:, None] * angle[None, :])
    psi = 2.0 / nodes * (basis @ values)
    psi[0] *= 0.5
    return psi


def halves(a):
    high = a.astype(np.float32).astype(ml_dtypes.bfloat16)
    low = (a - high.astype(np.float64)).astype(np.float32).astype(ml_dtypes.bfloat16)
    return high, low


def tables():
    psi = series()
    theta = np.pi / (2 * LEN) * np.outer(2 * np.arange(LEN) + 1, np.arange(LEN))
    forward = np.concatenate([np.cos(theta), -np.sin(theta)], 0)
    inverse = np.concatenate([np.cos(theta).T, -np.sin(theta).T], 1) / LEN
    to_bf16 = lambda a: a.astype(np.float32).astype(ml_dtypes.bfloat16)
    ends = np.concatenate(halves(psi[:, ::-1]), 0)
    th, tl = halves(forward @ psi.T)
    fh, fl = halves(psi.T)
    return (
        ends,
        to_bf16(forward),
        to_bf16(inverse),
        np.concatenate([th, tl, th], 1),
        np.concatenate([fh, fl, fh], 1),
    )


def split(a):
    high = a.astype(BF16)
    low = (a - high.astype(F32)).astype(BF16)
    return high, low


def dot(a, b):
    return jnp.dot(a, b, preferred_element_type=F32)


def kernel(
    order, blocks, prefix, suffix, gates, rates, residues, gain,
    ends_h, forward_h, inverse_h, taps_h, far_h,
    out,
    x, gt, near, outb, rate_v, res_v, gain_v,
    ends, forward, inverse, taps, fart,
    idx_v, idx_s,
    relay, zrel, tt, coef, step1, dec1, dec2, dec2s, pw,
    mid, spec, prod, hr, hi, hb, grel, gb,
    send1, recv1, incoming, send2, recv2, acc, ss, rss,
    sem_small, sem_x, sem_gate, sem_const, sem_idx, sem_out,
    s1, r1, s2, r2, s3, r3,
):
    me = lax.axis_index("ctx")
    mc = lax.axis_index("ch")

    small = [
        pltpu.make_async_copy(rates, rate_v, sem_small.at[0]),
        pltpu.make_async_copy(residues, res_v, sem_small.at[1]),
        pltpu.make_async_copy(ends_h, ends, sem_small.at[2]),
    ]
    for copy in small:
        copy.start()
    xcopies = []
    for c in range(6):
        src = prefix if c < 2 else suffix
        row = (c if c < 2 else c - 2) * LEN
        xcopies.append(
            pltpu.make_async_copy(src.at[pl.ds(row, LEN)], x.at[pl.ds(c * LEN, LEN)], sem_x.at[c])
        )
    for copy in xcopies:
        copy.start()
    consts = [
        pltpu.make_async_copy(a, b, sem_const.at[i])
        for i, (a, b) in enumerate(
            [(taps_h, taps), (forward_h, forward), (inverse_h, inverse), (far_h, fart), (gain, gain_v)]
        )
    ]
    for copy in consts:
        copy.start()
    gate_copy = pltpu.make_async_copy(gates, gt, sem_gate)
    gate_copy.start()

    barrier = pltpu.get_barrier_semaphore()

    @pl.loop(1, CTX)
    def _(r):
        pl.semaphore_signal(
            barrier, inc=1, device_id=(lax.rem(me + r, CTX), mc), device_id_type=MESH
        )

    @pl.loop(1, CH)
    def _(r):
        pl.semaphore_signal(
            barrier, inc=1, device_id=(me, lax.rem(mc + r, CH)), device_id_type=MESH
        )

    lane = lax.broadcasted_iota(jnp.int32, (8, 128), 1)

    def place(s, value):
        row = 3 * (s // 2) + 1 + s % 2
        return jnp.where(lane == order[s], row, value)

    idx_v[...] = lax.fori_loop(0, 2 * CTX, place, jnp.zeros((8, 128), jnp.int32), unroll=8)
    idx_copy = pltpu.make_async_copy(idx_v, idx_s, sem_idx)
    idx_copy.start()

    for copy in small:
        copy.wait()

    def spread(read):
        for g in range(2):
            for l in range(TILES):
                relay[pl.ds(g * 64 + l * 8, 8), :] = read(g, l)

    def mode(m):
        return relay[pl.ds(m // 8 * 64 + m % 8, 8, stride=8), :]

    live = blocks[0]
    gap = jnp.maximum(live - 1 - me, 0).astype(F32) * (2.0 * LEN)
    alive = jnp.where(me < live, 1.0, 0.0).astype(F32)
    spread(lambda g, l: rate_v[pl.ds(g * 8, 8), pl.ds(l * 128, 128)])
    for m in range(MODES):
        rate = mode(m)
        step1[m] = jnp.exp(-rate)
        d1 = jnp.exp(rate * (-1.0 * LEN))
        dec1[m] = d1
        d2 = jnp.exp(rate * (-2.0 * LEN))
        dec2[m] = d2
        dec2s[2 * m] = d2[:4]
        dec2s[2 * m + 1] = d2[4:]
        pw[m] = jnp.exp(rate * -gap) * alive
        coef[m] = jnp.sqrt(2.0 * rate)
        s = rate * (1.0 / RATE_HALF) - 1.0
        older, newer = jnp.ones_like(s), s
        tt[m, 0] = older
        tt[m, 1] = newer
        for k in range(2, ORD):
            older, newer = newer, 2.0 * s * newer - older
            tt[m, k] = newer
    spread(lambda g, l: res_v[pl.ds(g * 8, 8), pl.ds(l * 128, 128)])
    for m in range(MODES):
        coef[m] = coef[m] * mode(m)

    for c in range(6):
        xcopies[c].wait()
        for n in range(4):
            z = dot(ends[...], x[pl.ds(c * LEN, LEN), pl.ds(n * 256, 256)])
            z = z[:ORD] + z[ORD:]
            for g in range(2):
                for h in range(2):
                    zrel[c, pl.ds(g * 64 + (2 * n + h) * 8, 8), :] = z[
                        g * 8 : g * 8 + 8, h * 128 : h * 128 + 128
                    ]

    @pl.loop(0, MODES)
    def _(m):
        e = [None] * 6
        for k in range(ORD):
            t = tt[m, k]
            for c in range(6):
                term = t * zrel[c, pl.ds(k // 8 * 64 + k % 8, 8, stride=8), :]
                e[c] = term if k == 0 else e[c] + term
        d1 = dec1[m]
        mid[0, m] = e[2]
        mid[1, m] = e[4]
        full = [(e[0] * d1 + e[1]) * pw[m], e[2] * d1 + e[3], e[4] * d1 + e[5]]
        for j in range(3):
            send1[2 * m, j] = full[j][:4]
            send1[2 * m + 1, j] = full[j][4:]

    pl.semaphore_wait(barrier, CTX - 1 + CH - 1)

    @pl.loop(1, CTX)
    def _(r):
        to = lax.rem(me + r, CTX)
        pltpu.make_async_remote_copy(
            src_ref=send1.at[to], dst_ref=recv1.at[pl.ds(3 * me, 3)], send_sem=s1, recv_sem=r1,
            device_id=(to, mc), device_id_type=MESH,
        ).start()

    for j in range(3):
        recv1[3 * me + j] = send1[me, j]

    for copy in consts:
        copy.wait()

    def natural(values, write):
        for k in range(ORD):
            grel[pl.ds(k * 8, 8), :] = values(k)
        for l in range(TILES):
            high, low = split(grel[pl.ds(l, ORD, stride=8), :])
            write(l, jnp.concatenate([high, high, low], 0))

    def tap_term(k):
        total = tt[0, k] * coef[0]
        for m in range(1, MODES):
            total = total + tt[m, k] * coef[m]
        return total

    def put_taps(l, rows):
        hb[:, pl.ds(l * 128, 128)] = rows

    natural(tap_term, put_taps)

    @pl.loop(0, 4)
    def _(n):
        cols = pl.ds(pl.multiple_of(n * 256, 256), 256)
        both = dot(taps[...], hb[:, cols])
        hr[:, cols] = both[:LEN]
        hi[:, cols] = both[LEN:]

    def near_tile(i):
        c, n = i // 4, i % 4
        cols = pl.ds(pl.multiple_of(n * 256, 256), 256)
        rows = pl.ds(pl.multiple_of(c * LEN, LEN), LEN)
        spec[...] = dot(forward[...], x[pl.ds(pl.multiple_of((c + 2) * LEN, LEN), LEN), cols])
        xr, xi = spec[pl.ds(0, LEN), :], spec[pl.ds(LEN, LEN), :]
        tr, ti = hr[:, cols], hi[:, cols]
        prod[pl.ds(0, LEN), :] = (xr * tr - xi * ti).astype(BF16)
        prod[pl.ds(LEN, LEN), :] = (xr * ti + xi * tr).astype(BF16)
        near[rows, cols] = dot(inverse[...], prod[...])

    pl.loop(0, 8)(near_tile)

    pltpu.make_async_copy(
        recv1.at[pl.ds(0, 3 * (CTX - 1))], recv1.at[pl.ds(0, 3 * (CTX - 1))], r1
    ).wait()
    idx_copy.wait()
    parts = [recv1[3 * i] for i in range(4)]
    for i in range(4, CTX):
        parts[i % 4] = parts[i % 4] + recv1[3 * i]
    state = (parts[0] + parts[1]) + (parts[2] + parts[3])
    a = dec2s[me]
    aa = a * a
    for j in range(CTX):
        first, second = [recv1[idx_s[0, 2 * j + q]] for q in range(2)]
        incoming[2 * j] = state
        incoming[2 * j + 1] = a * state + first
        state = aa * state + (a * first + second)
    for s in range(2 * CTX):
        send2[s // 2, s % 2] = incoming[order[s]]

    @pl.loop(1, CTX)
    def _(r):
        to = lax.rem(me + r, CTX)
        pltpu.make_async_remote_copy(
            src_ref=send2.at[to], dst_ref=recv2.at[me], send_sem=s2, recv_sem=r2,
            device_id=(to, mc), device_id_type=MESH,
        ).start()

    for q in range(2):
        recv2[me, q] = send2[me, q]

    pl.loop(8, 16)(near_tile)

    gate_copy.wait()
    pltpu.make_async_copy(recv2.at[pl.ds(0, CTX - 1)], recv2.at[pl.ds(0, CTX - 1)], r2).wait()

    @pl.loop(0, MODES)
    def _(m):
        scale = coef[m] * step1[m]
        for q in range(2):
            state = jnp.concatenate([recv2[2 * m, q], recv2[2 * m + 1, q]], 0)
            spread_g = state * scale
            zrel[2 * q, pl.ds(pl.multiple_of(m * 8, 8), 8), :] = spread_g
            zrel[2 * q + 1, pl.ds(pl.multiple_of(m * 8, 8), 8), :] = (
                state * dec1[m] + mid[q, m]
            ) * scale

    @pl.loop(0, ORD)
    def _(k):
        g = [None] * 4
        for m in range(MODES):
            t = tt[m, k]
            for c in range(4):
                term = t * zrel[c, pl.ds(m * 8, 8), :]
                g[c] = term if m == 0 else g[c] + term
        for c in range(4):
            gb[c, pl.ds(pl.multiple_of(k * 8, 8), 8), :] = g[c]

    ones = jnp.ones((8, 128), BF16)
    for c in range(4):
        rows = pl.ds(c * LEN, LEN)

        def put_far(l, value):
            hb[:, pl.ds(l * 128, 128)] = value

        natural(lambda k: gb[c, pl.ds(k * 8, 8), :], put_far)
        for n in range(4):
            cols = pl.ds(n * 256, 256)
            value = near[rows, cols] + dot(fart[...], hb[:, cols])
            value = value * gt[rows, cols].astype(F32)
            near[rows, cols] = value
            square = value * value
            square = square[:, :128] + square[:, 128:]
            acc[...] = square if n == 0 else acc[...] + square
        high, low = split(acc[...])
        dims = (((1,), (1,)), ((), ()))
        sums = lax.dot_general(ones, high, dims, preferred_element_type=F32)
        sums = sums + lax.dot_general(ones, low, dims, preferred_element_type=F32)
        ss[pl.ds(2 * c, 1), :] = sums[:1, :128]
        ss[pl.ds(2 * c + 1, 1), :] = sums[:1, 128:]

    @pl.loop(1, CH)
    def _(r):
        to = lax.rem(mc + r, CH)
        pltpu.make_async_remote_copy(
            src_ref=ss, dst_ref=rss.at[mc], send_sem=s3, recv_sem=r3,
            device_id=(me, to), device_id_type=MESH,
        ).start()

    rss[mc] = ss[...]
    pltpu.make_async_copy(rss.at[pl.ds(0, CH - 1)], rss.at[pl.ds(0, CH - 1)], r3).wait()
    total = (rss[0] + rss[1]) + (rss[2] + rss[3])
    factor = lax.rsqrt(total * (1.0 / (CH * CHANS)) + EPS)
    for g in range(8):
        rows = pl.ds(g * 128, 128)
        column = jnp.transpose(jnp.broadcast_to(factor[g : g + 1, :], (128, 128)))
        for l in range(TILES):
            cols = pl.ds(l * 128, 128)
            outb[rows, cols] = (near[rows, cols] * column * gain_v[:, cols]).astype(BF16)
        pltpu.make_async_copy(outb.at[rows], out.at[rows], sem_out.at[g]).start()

    for g in range(8):
        rows = pl.ds(g * 128, 128)
        pltpu.make_async_copy(outb.at[rows], out.at[rows], sem_out.at[g]).wait()
    pltpu.make_async_copy(send1.at[pl.ds(0, CTX - 1)], send1.at[pl.ds(0, CTX - 1)], s1).wait()
    pltpu.make_async_copy(send2.at[pl.ds(0, CTX - 1)], send2.at[pl.ds(0, CTX - 1)], s2).wait()
    pltpu.make_async_copy(rss.at[pl.ds(0, CH - 1)], rss.at[pl.ds(0, CH - 1)], s3).wait()


def local(prefix, suffix, gates, rates, residues, gain, order, blocks):
    consts = [jnp.asarray(a) for a in tables()]
    hbm = pl.BlockSpec(memory_space=pl.ANY)
    smem = pl.BlockSpec(memory_space=pltpu.SMEM)
    vmem = pltpu.VMEM
    dma = pltpu.SemaphoreType.DMA
    scratch = [
        vmem((6 * LEN, CHANS), BF16),
        vmem((4 * LEN, CHANS), BF16),
        vmem((4 * LEN, CHANS), F32),
        vmem((4 * LEN, CHANS), BF16),
        vmem((MODES, CHANS), F32),
        vmem((MODES, CHANS), F32),
        vmem((1, CHANS), F32),
        vmem((2 * ORD, LEN), BF16),
        vmem((2 * LEN, LEN), BF16),
        vmem((LEN, 2 * LEN), BF16),
        vmem((2 * LEN, 3 * ORD), BF16),
        vmem((LEN, 3 * ORD), BF16),
        vmem((8, 128), jnp.int32),
        pltpu.SMEM((8, 128), jnp.int32),
        vmem((128, 128), F32),
        vmem((6, 128, 128), F32),
        vmem((MODES, ORD, 8, 128), F32),
        vmem((MODES, 8, 128), F32),
        vmem((MODES, 8, 128), F32),
        vmem((MODES, 8, 128), F32),
        vmem((MODES, 8, 128), F32),
        vmem((2 * MODES, 4, 128), F32),
        vmem((MODES, 8, 128), F32),
        vmem((2, MODES, 8, 128), F32),
        vmem((2 * LEN, 256), F32),
        vmem((2 * LEN, 256), BF16),
        vmem((LEN, CHANS), F32),
        vmem((LEN, CHANS), F32),
        vmem((3 * ORD, CHANS), BF16),
        vmem((128, 128), F32),
        vmem((4, 128, 128), F32),
        vmem((CTX, 3, 4, 128), F32),
        vmem((3 * CTX, 4, 128), F32),
        vmem((2 * CTX, 4, 128), F32),
        vmem((CTX, 2, 4, 128), F32),
        vmem((CTX, 2, 4, 128), F32),
        vmem((LEN, 128), F32),
        vmem((8, 128), F32),
        vmem((CH, 8, 128), F32),
        dma((3,)),
        dma((6,)),
        dma,
        dma((5,)),
        dma,
        dma((8,)),
        dma, dma, dma, dma, dma, dma,
    ]
    return pl.pallas_call(
        kernel,
        out_shape=jax.ShapeDtypeStruct((4 * LEN, CHANS), BF16),
        in_specs=[smem, smem] + [hbm] * 11,
        out_specs=hbm,
        scratch_shapes=scratch,
        compiler_params=pltpu.CompilerParams(
            collective_id=0, has_side_effects=True, vmem_limit_bytes=48 * 1024 * 1024
        ),
        cost_estimate=pl.CostEstimate(
            flops=6_000_000_000, bytes_accessed=8_000_000, transcendentals=100_000
        ),
    )(order, blocks, prefix, suffix, gates, rates, residues, gain[None, :], *consts)


def solution(mesh):
    return jax.shard_map(
        local,
        mesh=mesh,
        in_specs=(
            P("ctx", "ch"),
            P("ctx", "ch"),
            P("ctx", "ch"),
            P(None, "ch"),
            P(None, "ch"),
            P("ch"),
            P(),
            P(),
        ),
        out_specs=P("ctx", "ch"),
        check_vma=False,
    )
```

time: 549 us -> 42.6 us (0.08); the launches traced: 540 us -> 42.1 us
  waiting for transfers between devices: 281 us -> 0 us
  matrix products: 136 us -> 0 us
  other arithmetic: 53.6 us -> 0 us
  Pallas kernels: 0 us -> 29.9 us
  local copies, waits for them, and re-layouts: 39.2 us -> 11.5 us
  blocking collectives: 15.7 us -> 0 us
  between operations: 14.7 us -> 0.68 us
    psum x1 -> x0, waiting for transfers between devices: 281 us -> none  [local(): prefix_total = lax.psum(local_total, 'ctx')]
    dot_general x7 -> x0, matrix products: 136 us -> none  [the longest x1 32.3 us: local(): near = jnp.einsum('tk,bkc->btc', inverse, product, precision=HIGH)]
    pallas_call x0 -> x1, Pallas kernels: none -> 29.9 us  [local(): pl.pallas_call(kernel, out_shape=jax.ShapeDtypeStruct((4 * LEN, CHANS), B...]
    neg x2 -> x0, other arithmetic: 18.4 us -> none  [the longest x1 9.23 us: local(): forward = jnp.concatenate([jnp.cos(phase), -jnp.sin(phase)], 0)]
    psum x1 -> x0, blocking collectives: 15.7 us -> none  [local(): squares = lax.psum(jnp.sum(gated * gated, axis=1), 'ch')]
    exp x2 -> x0, other arithmetic: 13.4 us -> none  [the longest x1 11.4 us: local(): base = jnp.exp(-rates[:, None, :] * steps[None, :, None])]
    rev x1 -> x0, local copies, waits for them, and re-layouts: 13.1 us -> none  [local(): reverse = base[:, :sub_len][:, ::-1]]
    sub x2 -> x0, other arithmetic: 11.2 us -> none  [the longest x1 11.2 us: local(): real_x * real_h - imag_x * imag_h]
  transfers between devices with their start and end apart: 2 -> 0, of which waited for: 1 -> 0; matrix products, arithmetic and copies ran while one was open for 19% -> 0% of each run, Pallas kernels for 0% -> 0%
where the time goes in v1:
time: 42.6 us; the launch traced here: 42.1 us
  Pallas kernels  29.9 us (70%)
  local copies, waits for them, and re-layouts  11.5 us (27%)
  between operations  0.68 us (2%)
    pallas_call x1, Pallas kernels, local(): pl.pallas_call(kernel, out_shape=jax.ShapeDtypeStruct((4 * LEN, CHANS), B...  29.9 us
    unnamed x23, local copies, waits for them, and re-layouts  11.5 us

profile of v1, /device:TPU:1, one launch (start us, length us, event | category | flops | bytes accessed | tf_op | source)
XLA Modules:
  0.0 42.1 jit_solution(13112372675941394206)
XLA Ops:
  0.7 0.0 copy-start
  0.7 1.6 %copy-done = bf16[1024,1024]{1,0:T(8,128)(2,1)S(1)} copy-done((bf16[1024,1024]{1,0:T(8,128)(2,1)S(1)}, bf16[1024,1024]{1,0:T(8,128)(2,1)}, u32[]{:S(2)}) %copy-start) | copy-done | bytes 2097176
  2.2 0.0 copy-start.1
  2.2 1.2 %copy-done.1 = bf16[512,1024]{1,0:T(8,128)(2,1)S(1)} copy-done((bf16[512,1024]{1,0:T(8,128)(2,1)S(1)}, bf16[512,1024]{1,0:T(8,128)(2,1)}, u32[]{:S(2)}) %copy-start.1) | copy-done | bytes 1048600
  3.5 0.0 copy-start.2
  3.5 0.8 %copy-done.2 = f32[16,1024]{1,0:T(8,128)S(1)} copy-done((f32[16,1024]{1,0:T(8,128)S(1)}, f32[16,1024]{1,0:T(8,128)}, u32[]{:S(2)}) %copy-start.2) | copy-done | bytes 65560
  4.3 0.0 copy-start.3
  4.3 0.8 %copy-done.3 = f32[16,1024]{1,0:T(8,128)S(1)} copy-done((f32[16,1024]{1,0:T(8,128)S(1)}, f32[16,1024]{1,0:T(8,128)}, u32[]{:S(2)}) %copy-start.3) | copy-done | bytes 65560
  5.1 0.0 copy-start.4
  5.2 0.7 %copy-done.4 = f32[1024]{0:T(1024)S(1)} copy-done((f32[1024]{0:T(1024)S(1)}, f32[1024]{0:T(1024)}, u32[]{:S(2)}) %copy-start.4) | copy-done | bytes 4120
  5.8 0.0 copy-start.5
  5.8 0.7 %copy-done.5 = s32[64]{0:T(128)S(1)} copy-done((s32[64]{0:T(128)S(1)}, s32[64]{0:T(128)}, u32[]{:S(2)}) %copy-start.5) | copy-done | bytes 280
  6.5 0.0 copy-start.6
  6.5 0.9 %copy-done.6 = bf16[256,512]{1,0:T(8,128)(2,1)S(1)} copy-done((bf16[256,512]{1,0:T(8,128)(2,1)S(1)}, bf16[256,512]{1,0:T(8,128)(2,1)}, u32[]{:S(2)}) %copy-start.6) | copy-done | bytes 262168
  7.4 0.0 copy-start.7
  7.4 0.9 %copy-done.7 = bf16[512,256]{1,0:T(8,128)(2,1)S(1)} copy-done((bf16[512,256]{1,0:T(8,128)(2,1)S(1)}, bf16[512,256]{1,0:T(8,128)(2,1)}, u32[]{:S(2)}) %copy-start.7) | copy-done | bytes 262168
  8.4 0.0 copy-start.8
  8.4 0.9 %copy-done.8 = bf16[512,48]{1,0:T(8,128)(2,1)S(1)} copy-done((bf16[512,48]{1,0:T(8,128)(2,1)S(1)}, bf16[512,48]{1,0:T(8,128)(2,1)}, u32[]{:S(2)}) %copy-start.8) | copy-done | bytes 49176
  9.3 0.0 copy-start.9
  9.3 0.8 %copy-done.9 = bf16[256,48]{1,0:T(8,128)(2,1)S(1)} copy-done((bf16[256,48]{1,0:T(8,128)(2,1)S(1)}, bf16[256,48]{1,0:T(8,128)(2,1)}, u32[]{:S(2)}) %copy-start.9) | copy-done | bytes 24600
  10.1 0.0 copy-start.10
  10.1 0.7 %copy-done.10 = bf16[32,256]{1,0:T(8,128)(2,1)S(1)} copy-done((bf16[32,256]{1,0:T(8,128)(2,1)S(1)}, bf16[32,256]{1,0:T(8,128)(2,1)}, u32[]{:S(2)}) %copy-start.10) | copy-done | bytes 16408
  10.9 29.9 %shard_map.127 = bf16[1024,1024]{1,0:T(8,128)(2,1)S(1)} custom-call(s32[64]{0:T(128)S(1)} %copy-done.5, s32[1]{0:T(128)S(6)} %copy.15.blocks, bf16[512,1024]{1,0:T(8,128)(2,1)S(1)} %copy-done.1, bf16[1024,1024]{1,0:T(8,128)(2,1)S(1)} %copy-done, bf16[1024,1024]{1,0:T(8,128)(2,1)} %gates.1, f32[16,1024]{1,0:T(8,128)S(1)} %copy-done.2, ...), custom_call_target="tpu_custom_call" | custom-call | flops 6000000000 | bytes 8000000 | tf_op jit(solution)/shard_map/pallas_call | solution.py:418
  40.8 1.3 %copy.16 = bf16[1024,1024]{1,0:T(8,128)(2,1)} copy(bf16[1024,1024]{1,0:T(8,128)(2,1)S(1)} %shard_map.127) | data formatting | bytes 4194304
Async XLA Ops:
  0.7 1.6 %copy-start = (bf16[1024,1024]{1,0:T(8,128)(2,1)S(1)}, bf16[1024,1024]{1,0:T(8,128)(2,1)}, u32[]{:S(2)}) copy-start(bf16[1024,1024]{1,0:T(8,128)(2,1)} %suffix.1) | copy-start | bytes 6291460
  2.2 1.2 %copy-start.1 = (bf16[512,1024]{1,0:T(8,128)(2,1)S(1)}, bf16[512,1024]{1,0:T(8,128)(2,1)}, u32[]{:S(2)}) copy-start(bf16[512,1024]{1,0:T(8,128)(2,1)} %prefix.1) | copy-start | bytes 3145732
  3.5 0.8 %copy-start.2 = (f32[16,1024]{1,0:T(8,128)S(1)}, f32[16,1024]{1,0:T(8,128)}, u32[]{:S(2)}) copy-start(f32[16,1024]{1,0:T(8,128)} %rates.1) | copy-start | bytes 196612
  4.3 0.8 %copy-start.3 = (f32[16,1024]{1,0:T(8,128)S(1)}, f32[16,1024]{1,0:T(8,128)}, u32[]{:S(2)}) copy-start(f32[16,1024]{1,0:T(8,128)} %residues.1) | copy-start | bytes 196612
  5.1 0.7 %copy-start.4 = (f32[1024]{0:T(1024)S(1)}, f32[1024]{0:T(1024)}, u32[]{:S(2)}) copy-start(f32[1024]{0:T(1024)} %param.18) | copy-start | bytes 12292
  5.8 0.7 %copy-start.5 = (s32[64]{0:T(128)S(1)}, s32[64]{0:T(128)}, u32[]{:S(2)}) copy-start(s32[64]{0:T(128)} %order.1) | copy-start | bytes 772
  6.5 0.9 %copy-start.6 = (bf16[256,512]{1,0:T(8,128)(2,1)S(1)}, bf16[256,512]{1,0:T(8,128)(2,1)}, u32[]{:S(2)}) copy-start(bf16[256,512]{1,0:T(8,128)(2,1)} %constant.12.clone.inverse_h) | copy-start | bytes 786436
  7.4 0.9 %copy-start.7 = (bf16[512,256]{1,0:T(8,128)(2,1)S(1)}, bf16[512,256]{1,0:T(8,128)(2,1)}, u32[]{:S(2)}) copy-start(bf16[512,256]{1,0:T(8,128)(2,1)} %constant.11.clone.forward_h) | copy-start | bytes 786436
  8.4 0.9 %copy-start.8 = (bf16[512,48]{1,0:T(8,128)(2,1)S(1)}, bf16[512,48]{1,0:T(8,128)(2,1)}, u32[]{:S(2)}) copy-start(bf16[512,48]{1,0:T(8,128)(2,1)} %constant.13.clone.taps_h) | copy-start | bytes 147460
  9.3 0.8 %copy-start.9 = (bf16[256,48]{1,0:T(8,128)(2,1)S(1)}, bf16[256,48]{1,0:T(8,128)(2,1)}, u32[]{:S(2)}) copy-start(bf16[256,48]{1,0:T(8,128)(2,1)} %constant.14.clone.far_h) | copy-start | bytes 73732
  10.1 0.7 %copy-start.10 = (bf16[32,256]{1,0:T(8,128)(2,1)S(1)}, bf16[32,256]{1,0:T(8,128)(2,1)}, u32[]{:S(2)}) copy-start(bf16[32,256]{1,0:T(8,128)(2,1)} %constant.10.clone.ends_h) | copy-start | bytes 49156

commit v2 on v1

v2 whole, which is shorter than its diff:
```python
import functools

import jax
import jax.numpy as jnp
import ml_dtypes
import numpy as np
from jax import lax
from jax.experimental import pallas as pl
from jax.experimental.pallas import tpu as pltpu
from jax.sharding import PartitionSpec as P

MESH = pl.DeviceIdType.MESH
F32 = jnp.float32
BF16 = jnp.bfloat16

LEN = 256
ORD = 16
MODES = 16
CTX = 32
CH = 4
CHANS = 1024
TILES = CHANS // 128
RATE_HALF = 1.0 / 48.0
EPS = 1e-6


def series():
    nodes = 64
    angle = np.pi * (np.arange(nodes) + 0.5) / nodes
    rate = RATE_HALF * (1.0 + np.cos(angle))
    values = np.exp(-rate[:, None] * np.arange(LEN)[None, :])
    basis = np.cos(np.arange(ORD)[:, None] * angle[None, :])
    psi = 2.0 / nodes * (basis @ values)
    psi[0] *= 0.5
    return psi


def halves(a):
    high = a.astype(np.float32).astype(ml_dtypes.bfloat16)
    low = (a - high.astype(np.float64)).astype(np.float32).astype(ml_dtypes.bfloat16)
    return high, low


def tables():
    psi = series()
    theta = np.pi / (2 * LEN) * np.outer(2 * np.arange(LEN) + 1, np.arange(LEN))
    forward = np.concatenate([np.cos(theta), -np.sin(theta)], 0)
    inverse = np.concatenate([np.cos(theta).T, -np.sin(theta).T], 1) / LEN
    to_bf16 = lambda a: a.astype(np.float32).astype(ml_dtypes.bfloat16)
    ends = np.concatenate(halves(psi[:, ::-1]), 0)
    th, tl = halves(forward @ psi.T)
    fh, fl = halves(psi.T)
    arrays = (
        ends,
        np.concatenate([th, tl, th], 1),
        to_bf16(forward),
        to_bf16(inverse),
        np.concatenate([fh, fl, fh], 1),
    )
    slabs, places, row = [], [], 0
    for a in arrays:
        a = np.pad(a, ((0, 0), (0, -a.shape[1] % 128)))
        for col in range(0, a.shape[1], 128):
            slabs.append(a[:, col : col + 128])
            places.append((row, a.shape[0], col))
            row += a.shape[0]
    return np.concatenate(slabs, 0), places


def offsets():
    steps = [(dx, dz, dy) for dx in range(2) for dz in range(4) for dy in range(4)]
    hops = lambda s: 2 * s[0] + min(s[1], 4 - s[1]) + min(s[2], 4 - s[2])
    return sorted(steps[1:], key=hops, reverse=True)


def split(a):
    high = a.astype(BF16)
    low = (a - high.astype(F32)).astype(BF16)
    return high, low


def dot(a, b):
    return jnp.dot(a, b, preferred_element_type=F32)


def kernel(
    places,
    blocks, order_h, prefix, suffix, gates, rates, residues, gain, packed,
    out,
    order, x, gt, near, rate_v, res_v, gain_v,
    ends, forward, inverse, taps, fart,
    idx_v, idx_s,
    relay, zrel, zd, tt, rate_m, coef, step1, dec1, dec2s, pw,
    mid, spec, prod, hr, hi, hb, grel, gm, gb, hf,
    send1, recv1, incoming, send2, recv2, acc, ss, rss,
    sem_small, sem_x, sem_gate, sem_const, sem_idx,
    s1, r1, s2, r2, s3, r3,
):
    me = lax.axis_index("ctx")
    mc = lax.axis_index("ch")

    small = [
        pltpu.make_async_copy(rates, rate_v, sem_small.at[0]),
        pltpu.make_async_copy(residues, res_v, sem_small.at[1]),
        pltpu.make_async_copy(order_h, order, sem_small.at[2]),
    ]
    targets = [ends] * 2 + [taps] + [forward] * 2 + [inverse] * 4 + [fart]
    consts = [
        pltpu.make_async_copy(
            packed.at[pl.ds(row, count)], target.at[:, pl.ds(col, 128)], sem_const.at[i]
        )
        for i, ((row, count, col), target) in enumerate(zip(places, targets))
    ]
    consts.append(pltpu.make_async_copy(gain, gain_v, sem_const.at[len(consts)]))
    for copy in small + consts[:2]:
        copy.start()
    xcopies = []
    for c in range(6):
        src = prefix if c < 2 else suffix
        row = (c if c < 2 else c - 2) * LEN
        xcopies.append(
            pltpu.make_async_copy(src.at[pl.ds(row, LEN)], x.at[pl.ds(c * LEN, LEN)], sem_x.at[c])
        )
    for copy in xcopies:
        copy.start()

    barrier = pltpu.get_barrier_semaphore()
    xs = [lax.rem(me // 16 + d, 2) * 16 for d in range(2)]
    zs = [lax.rem(me // 4 + d, 4) * 4 for d in range(4)]
    ys = [lax.rem(me + d, 4) for d in range(4)]
    peers = [xs[dx] + zs[dz] + ys[dy] for dx, dz, dy in offsets()]
    others = [lax.rem(mc + r, CH) for r in (2, 3, 1)]
    for to in peers:
        pl.semaphore_signal(barrier, inc=1, device_id=(to, mc), device_id_type=MESH)
    for to in others:
        pl.semaphore_signal(barrier, inc=1, device_id=(me, to), device_id_type=MESH)

    for copy in consts[2:]:
        copy.start()
    gate_copy = pltpu.make_async_copy(gates, gt, sem_gate)
    gate_copy.start()

    for copy in small:
        copy.wait()

    def spread(read):
        for g in range(2):
            for l in range(TILES):
                relay[pl.ds(g * 64 + l * 8, 8), :] = read(g, l)

    def mode(m):
        return relay[pl.ds(m // 8 * 64 + m % 8, 8, stride=8), :]

    live = blocks[0]
    gap = jnp.maximum(live - 1 - me, 0).astype(F32) * (2.0 * LEN)
    alive = jnp.where(me < live, 1.0, 0.0).astype(F32)
    spread(lambda g, l: rate_v[pl.ds(g * 8, 8), pl.ds(l * 128, 128)])
    for m in range(MODES):
        rate = mode(m)
        rate_m[m] = rate
        dec1[m] = jnp.exp(rate * (-1.0 * LEN))
        pw[m] = jnp.exp(rate * -gap) * alive
        s = rate * (1.0 / RATE_HALF) - 1.0
        older, newer = jnp.ones_like(s), s
        tt[m, 0] = older
        tt[m, 1] = newer
        for k in range(2, ORD):
            older, newer = newer, 2.0 * s * newer - older
            tt[m, k] = newer

    for copy in consts[:2]:
        copy.wait()
    for c in range(6):
        xcopies[c].wait()
        for n in range(4):
            z = dot(ends[...], x[pl.ds(c * LEN, LEN), pl.ds(n * 256, 256)])
            z = z[:ORD] + z[ORD:]
            for g in range(2):
                for h in range(2):
                    zrel[c, pl.ds(g * 64 + (2 * n + h) * 8, 8), :] = z[
                        g * 8 : g * 8 + 8, h * 128 : h * 128 + 128
                    ]

    for c in range(6):
        for k in range(ORD):
            zd[c, k] = zrel[c, pl.ds(k // 8 * 64 + k % 8, 8, stride=8), :]

    @pl.loop(0, MODES, step=4)
    def _(first):
        e = [[None] * 6 for _ in range(4)]
        for k in range(ORD):
            z = [zd[c, k] for c in range(6)]
            for i in range(4):
                t = tt[first + i, k]
                for c in range(6):
                    e[i][c] = t * z[c] if k == 0 else e[i][c] + t * z[c]
        for i in range(4):
            m = first + i
            d1 = dec1[m]
            mid[0, m] = e[i][2]
            mid[1, m] = e[i][4]
            full = [
                (e[i][0] * d1 + e[i][1]) * pw[m],
                e[i][2] * d1 + e[i][3],
                e[i][4] * d1 + e[i][5],
            ]
            for j in range(3):
                send1[2 * m, j] = full[j][:4]
                send1[2 * m + 1, j] = full[j][4:]

    pl.semaphore_wait(barrier, CTX - 1 + CH - 1)

    for to in peers:
        pltpu.make_async_remote_copy(
            src_ref=send1.at[to], dst_ref=recv1.at[pl.ds(3 * me, 3)], send_sem=s1, recv_sem=r1,
            device_id=(to, mc), device_id_type=MESH,
        ).start()

    for j in range(3):
        recv1[3 * me + j] = send1[me, j]

    lane = lax.broadcasted_iota(jnp.int32, (8, 128), 1)

    def place(s, value):
        row = 3 * (s // 2) + 1 + s % 2
        return jnp.where(lane == order[s], row, value)

    idx_v[...] = lax.fori_loop(0, 2 * CTX, place, jnp.zeros((8, 128), jnp.int32), unroll=8)
    idx_copy = pltpu.make_async_copy(idx_v, idx_s, sem_idx)
    idx_copy.start()

    spread(lambda g, l: res_v[pl.ds(g * 8, 8), pl.ds(l * 128, 128)])
    for m in range(MODES):
        rate = rate_m[m]
        step1[m] = jnp.exp(-rate)
        d2 = jnp.exp(rate * (-2.0 * LEN))
        dec2s[2 * m] = d2[:4]
        dec2s[2 * m + 1] = d2[4:]
        coef[m] = jnp.sqrt(2.0 * rate) * mode(m)

    for copy in consts[2:]:
        copy.wait()

    def natural(tiles, rows):
        for l in range(TILES):
            high, low = split(tiles[pl.ds(l, ORD, stride=8), :])
            rows[:, pl.ds(l * 128, 128)] = jnp.concatenate([high, high, low], 0)

    @pl.loop(0, ORD, step=4)
    def _(first):
        total = [None] * 4
        for m in range(MODES):
            for i in range(4):
                term = tt[m, first + i] * coef[m]
                total[i] = term if m == 0 else total[i] + term
        for i in range(4):
            grel[pl.ds(pl.multiple_of((first + i) * 8, 8), 8), :] = total[i]

    natural(grel, hb)

    @pl.loop(0, 4)
    def _(n):
        cols = pl.ds(pl.multiple_of(n * 256, 256), 256)
        both = dot(taps[:, : 3 * ORD], hb[:, cols])
        hr[:, cols] = both[:LEN]
        hi[:, cols] = both[LEN:]

    def near_chunk(c):
        rows = pl.ds(pl.multiple_of(c * LEN, LEN), LEN)
        xrows = pl.ds(pl.multiple_of((c + 2) * LEN, LEN), LEN)
        cols = [pl.ds(n * 256, 256) for n in range(4)]
        low, high = pl.ds(0, LEN), pl.ds(LEN, LEN)

        def to_spectrum(n):
            spec[n] = dot(forward[...], x[xrows, cols[n]])

        to_spectrum(0)
        for n in range(4):
            if n < 3:
                to_spectrum(n + 1)
            xr, xi = spec[n, low, :], spec[n, high, :]
            tr, ti = hr[:, cols[n]], hi[:, cols[n]]
            prod[n, low, :] = (xr * tr - xi * ti).astype(BF16)
            prod[n, high, :] = (xr * ti + xi * tr).astype(BF16)
            near[rows, cols[n]] = dot(inverse[...], prod[n])

    pl.loop(0, 2)(near_chunk)

    pltpu.make_async_copy(
        recv1.at[pl.ds(0, 3 * (CTX - 1))], recv1.at[pl.ds(0, 3 * (CTX - 1))], r1
    ).wait()
    idx_copy.wait()
    parts = [recv1[3 * i] for i in range(4)]
    for i in range(4, CTX):
        parts[i % 4] = parts[i % 4] + recv1[3 * i]
    state = (parts[0] + parts[1]) + (parts[2] + parts[3])
    a = dec2s[me]
    aa = a * a
    for j in range(CTX):
        first, second = [recv1[idx_s[0, 2 * j + q]] for q in range(2)]
        incoming[2 * j] = state
        incoming[2 * j + 1] = a * state + first
        state = aa * state + (a * first + second)
    for s in range(2 * CTX):
        send2[s // 2, s % 2] = incoming[order[s]]

    for to in peers:
        pltpu.make_async_remote_copy(
            src_ref=send2.at[to], dst_ref=recv2.at[me], send_sem=s2, recv_sem=r2,
            device_id=(to, mc), device_id_type=MESH,
        ).start()

    for q in range(2):
        recv2[me, q] = send2[me, q]

    pl.loop(2, 4)(near_chunk)

    gate_copy.wait()
    pltpu.make_async_copy(recv2.at[pl.ds(0, CTX - 1)], recv2.at[pl.ds(0, CTX - 1)], r2).wait()

    for m in range(MODES):
        scale = coef[m] * step1[m]
        for q in range(2):
            state = jnp.concatenate([recv2[2 * m, q], recv2[2 * m + 1, q]], 0)
            gm[2 * q, m] = state * scale
            gm[2 * q + 1, m] = (state * dec1[m] + mid[q, m]) * scale

    @pl.loop(0, ORD, step=4)
    def _(first):
        g = [[None] * 4 for _ in range(4)]
        for m in range(MODES):
            u = [gm[c, m] for c in range(4)]
            for i in range(4):
                t = tt[m, first + i]
                for c in range(4):
                    g[i][c] = t * u[c] if m == 0 else g[i][c] + t * u[c]
        for i in range(4):
            for c in range(4):
                gb[c, pl.ds(pl.multiple_of((first + i) * 8, 8), 8), :] = g[i][c]

    for c in range(4):
        natural(gb.at[c], hf.at[c])

    ones = jnp.ones((8, 128), BF16)
    for c in range(4):
        rows = pl.ds(c * LEN, LEN)
        for n in range(4):
            cols = pl.ds(n * 256, 256)
            value = near[rows, cols] + dot(fart[:, : 3 * ORD], hf[c, :, cols])
            value = value * gt[rows, cols].astype(F32)
            near[rows, cols] = value
            square = value * value
            square = square[:, :128] + square[:, 128:]
            acc[c] = square if n == 0 else acc[c] + square
        high, low = split(acc[c])
        dims = (((1,), (1,)), ((), ()))
        sums = lax.dot_general(ones, high, dims, preferred_element_type=F32)
        sums = sums + lax.dot_general(ones, low, dims, preferred_element_type=F32)
        ss[c, pl.ds(0, 1), :] = sums[:1, :128]
        ss[c, pl.ds(1, 1), :] = sums[:1, 128:]
        for to in others:
            pltpu.make_async_remote_copy(
                src_ref=ss.at[c], dst_ref=rss.at[c, mc], send_sem=s3, recv_sem=r3.at[c],
                device_id=(me, to), device_id_type=MESH,
            ).start()
        rss[c, mc] = ss[c]

    for c in range(4):
        three = rss.at[c, pl.ds(0, CH - 1)]
        pltpu.make_async_copy(three, three, r3.at[c]).wait()
        total = (rss[c, 0] + rss[c, 1]) + (rss[c, 2] + rss[c, 3])
        factor = lax.rsqrt(total * (1.0 / (CH * CHANS)) + EPS)
        for g in range(2):
            rows = pl.ds(c * LEN + g * 128, 128)
            column = jnp.transpose(jnp.broadcast_to(factor[g : g + 1, :], (128, 128)))
            for l in range(TILES):
                cols = pl.ds(l * 128, 128)
                out[rows, cols] = (near[rows, cols] * column * gain_v[:, cols]).astype(BF16)

    pltpu.make_async_copy(send1.at[pl.ds(0, CTX - 1)], send1.at[pl.ds(0, CTX - 1)], s1).wait()
    pltpu.make_async_copy(send2.at[pl.ds(0, CTX - 1)], send2.at[pl.ds(0, CTX - 1)], s2).wait()
    pltpu.make_async_copy(rss.at[pl.ds(0, CH - 1)], rss.at[pl.ds(0, CH - 1)], s3).wait()


def local(prefix, suffix, gates, rates, residues, gain, order, blocks):
    packed, places = tables()
    hbm = pl.BlockSpec(memory_space=pltpu.HBM)
    vmem = pltpu.VMEM
    dma = pltpu.SemaphoreType.DMA
    scratch = [
        pltpu.SMEM((2 * CTX,), jnp.int32),
        vmem((6 * LEN, CHANS), BF16),
        vmem((4 * LEN, CHANS), BF16),
        vmem((4 * LEN, CHANS), F32),
        vmem((MODES, CHANS), F32),
        vmem((MODES, CHANS), F32),
        vmem((1, CHANS), F32),
        vmem((2 * ORD, LEN), BF16),
        vmem((2 * LEN, LEN), BF16),
        vmem((LEN, 2 * LEN), BF16),
        vmem((2 * LEN, 128), BF16),
        vmem((LEN, 128), BF16),
        vmem((8, 128), jnp.int32),
        pltpu.SMEM((8, 128), jnp.int32),
        vmem((128, 128), F32),
        vmem((6, 128, 128), F32),
        vmem((6, ORD, 8, 128), F32),
        vmem((MODES, ORD, 8, 128), F32),
        vmem((MODES, 8, 128), F32),
        vmem((MODES, 8, 128), F32),
        vmem((MODES, 8, 128), F32),
        vmem((MODES, 8, 128), F32),
        vmem((2 * MODES, 4, 128), F32),
        vmem((MODES, 8, 128), F32),
        vmem((2, MODES, 8, 128), F32),
        vmem((4, 2 * LEN, 256), F32),
        vmem((4, 2 * LEN, 256), BF16),
        vmem((LEN, CHANS), F32),
        vmem((LEN, CHANS), F32),
        vmem((3 * ORD, CHANS), BF16),
        vmem((128, 128), F32),
        vmem((4, MODES, 8, 128), F32),
        vmem((4, 128, 128), F32),
        vmem((4, 3 * ORD, CHANS), BF16),
        vmem((CTX, 3, 4, 128), F32),
        vmem((3 * CTX, 4, 128), F32),
        vmem((2 * CTX, 4, 128), F32),
        vmem((CTX, 2, 4, 128), F32),
        vmem((CTX, 2, 4, 128), F32),
        vmem((4, LEN, 128), F32),
        vmem((4, 2, 128), F32),
        vmem((4, CH, 2, 128), F32),
        dma((3,)),
        dma((6,)),
        dma,
        dma((len(places) + 1,)),
        dma,
        dma, dma, dma, dma, dma, dma((4,)),
    ]
    operands = (
        order, prefix, suffix, gates, rates, residues, gain[None, :], jnp.asarray(packed)
    )
    return pl.pallas_call(
        functools.partial(kernel, places),
        out_shape=pltpu.VMEM((4 * LEN, CHANS), BF16),
        in_specs=[pl.BlockSpec(memory_space=pltpu.SMEM)] + [hbm] * 8,
        out_specs=pl.BlockSpec(memory_space=pltpu.VMEM),
        scratch_shapes=scratch,
        compiler_params=pltpu.CompilerParams(
            collective_id=0, has_side_effects=True, vmem_limit_bytes=48 * 1024 * 1024
        ),
        cost_estimate=pl.CostEstimate(
            flops=6_000_000_000, bytes_accessed=8_000_000, transcendentals=100_000
        ),
    )(blocks, *(pltpu.with_memory_space_constraint(a, pltpu.HBM) for a in operands))


def solution(mesh):
    return jax.shard_map(
        local,
        mesh=mesh,
        in_specs=(
            P("ctx", "ch"),
            P("ctx", "ch"),
            P("ctx", "ch"),
            P(None, "ch"),
            P(None, "ch"),
            P("ch"),
            P(),
            P(),
        ),
        out_specs=P("ctx", "ch"),
        check_vma=False,
    )
```

time: 42.6 us -> 29.4 us (0.69)
  local copies, waits for them, and re-layouts: 11.5 us -> 1.32 us
  Pallas kernels: 29.9 us -> 27.3 us
    unnamed x23 -> x1, local copies, waits for them, and re-layouts: 11.5 us -> 1.32 us
    pallas_call x1, Pallas kernels: 29.9 us -> 27.3 us  [local(): pl.pallas_call(functools.partial(kernel, places), out_shape=pltpu.VMEM((4...]
where the time goes in v2:
time: 29.4 us; the launch traced here: 29.3 us
  Pallas kernels  27.3 us (93%)
  local copies, waits for them, and re-layouts  1.32 us (4%)
  between operations  0.66 us (2%)
    pallas_call x1, Pallas kernels, local(): pl.pallas_call(functools.partial(kernel, places), out_shape=pltpu.VMEM((4...  27.3 us
    unnamed x1, local copies, waits for them, and re-layouts  1.32 us

profile of v2, /device:TPU:1, one launch (start us, length us, event | category | flops | bytes accessed | tf_op | source)
XLA Modules:
  0.0 29.3 jit_solution(12186719268838436901)
XLA Ops:
  0.7 27.3 %shard_map.91 = bf16[1024,1024]{1,0:T(8,128)(2,1)S(1)} custom-call(s32[1]{0:T(128)S(6)} %copy.12.blocks, s32[64]{0:T(128)} %order_h.1, bf16[512,1024]{1,0:T(8,128)(2,1)} %prefix.1, bf16[1024,1024]{1,0:T(8,128)(2,1)} %suffix.1, bf16[1024,1024]{1,0:T(8,128)(2,1)} %gates.1, f32[16,1024]{1,0:T(8,128)} %rates.1, f32[16,1024]{1,0:T(8,128)} %residues.1, ...), custom_call_target="tpu_custom_call" | custom-call | flops 6000000000 | bytes 8000000 | tf_op jit(solution)/shard_map/pallas_call | solution.py:443
  27.9 1.3 %copy.11 = bf16[1024,1024]{1,0:T(8,128)(2,1)} copy(bf16[1024,1024]{1,0:T(8,128)(2,1)S(1)} %shard_map.91) | data formatting | bytes 4194304

commit v3 on v2

--- a/solution.py
+++ b/solution.py
@@ -67,10 +67,18 @@
     return np.concatenate(slabs, 0), places
 
 
-def offsets():
-    steps = [(dx, dz, dy) for dx in range(2) for dz in range(4) for dy in range(4)]
-    hops = lambda s: 2 * s[0] + min(s[1], 4 - s[1]) + min(s[2], 4 - s[2])
-    return sorted(steps[1:], key=hops, reverse=True)
+def place_of(ctx):
+    return ctx // 16, ctx // 4 % 4, ctx % 4
+
+
+def lateness(ctx):
+    x, z, y = place_of(ctx)
+    return 1.5 * x + 1.0 * z + 0.85 * y
+
+
+BY_START = sorted(range(CTX), key=lateness)
+SERVERS = BY_START[:16]
+PER = MODES // len(SERVERS)
 
 
 def split(a):
@@ -90,7 +98,7 @@
     order, x, gt, near, rate_v, res_v, gain_v,
     ends, forward, inverse, taps, fart,
     idx_v, idx_s,
-    relay, zrel, zd, tt, rate_m, coef, step1, dec1, dec2s, pw,
+    relay, zrel, zd, tt, rate_m, coef, step1, dec1, dec2, pw,
     mid, spec, prod, hr, hi, hb, grel, gm, gb, hf,
     send1, recv1, incoming, send2, recv2, acc, ss, rss,
     sem_small, sem_x, sem_gate, sem_const, sem_idx,
@@ -125,13 +133,19 @@
         copy.start()
 
     barrier = pltpu.get_barrier_semaphore()
-    xs = [lax.rem(me // 16 + d, 2) * 16 for d in range(2)]
-    zs = [lax.rem(me // 4 + d, 4) * 4 for d in range(4)]
-    ys = [lax.rem(me + d, 4) for d in range(4)]
-    peers = [xs[dx] + zs[dz] + ys[dy] for dx, dz, dy in offsets()]
     others = [lax.rem(mc + r, CH) for r in (2, 3, 1)]
-    for to in peers:
-        pl.semaphore_signal(barrier, inc=1, device_id=(to, mc), device_id_type=MESH)
+    serves = functools.reduce(jnp.logical_or, [me == ctx for ctx in SERVERS])
+    number = sum(jnp.where(me == ctx, i, 0) for i, ctx in enumerate(SERVERS))
+    replies = len(SERVERS) - jnp.where(serves, 1, 0)
+
+    @pl.when(serves)
+    def _():
+        for to in BY_START:
+
+            @pl.when(me != to)
+            def _():
+                pl.semaphore_signal(barrier, inc=1, device_id=(to, mc), device_id_type=MESH)
+
     for to in others:
         pl.semaphore_signal(barrier, inc=1, device_id=(me, to), device_id_type=MESH)
 
@@ -205,25 +219,28 @@
                 e[i][4] * d1 + e[i][5],
             ]
             for j in range(3):
-                send1[2 * m, j] = full[j][:4]
-                send1[2 * m + 1, j] = full[j][4:]
-
-    pl.semaphore_wait(barrier, CTX - 1 + CH - 1)
-
-    for to in peers:
-        pltpu.make_async_remote_copy(
-            src_ref=send1.at[to], dst_ref=recv1.at[pl.ds(3 * me, 3)], send_sem=s1, recv_sem=r1,
-            device_id=(to, mc), device_id_type=MESH,
-        ).start()
-
-    for j in range(3):
-        recv1[3 * me + j] = send1[me, j]
+                send1[m, j] = full[j]
+
+    pl.semaphore_wait(barrier, replies + CH - 1)
+
+    for i, to in enumerate(SERVERS):
+        part = send1.at[pl.ds(i * PER, PER)]
+
+        @pl.when(me != to)
+        def _():
+            pltpu.make_async_remote_copy(
+                src_ref=part, dst_ref=recv1.at[me], send_sem=s1, recv_sem=r1,
+                device_id=(to, mc), device_id_type=MESH,
+            ).start()
+
+        @pl.when(me == to)
+        def _():
+            recv1[me] = part[...]
 
     lane = lax.broadcasted_iota(jnp.int32, (8, 128), 1)
 
     def place(s, value):
-        row = 3 * (s // 2) + 1 + s % 2
-        return jnp.where(lane == order[s], row, value)
+        return jnp.where(lane == order[s], s, value)
 
     idx_v[...] = lax.fori_loop(0, 2 * CTX, place, jnp.zeros((8, 128), jnp.int32), unroll=8)
     idx_copy = pltpu.make_async_copy(idx_v, idx_s, sem_idx)
@@ -234,8 +251,7 @@
         rate = rate_m[m]
         step1[m] = jnp.exp(-rate)
         d2 = jnp.exp(rate * (-2.0 * LEN))
-        dec2s[2 * m] = d2[:4]
-        dec2s[2 * m + 1] = d2[4:]
+        dec2[m] = d2
         coef[m] = jnp.sqrt(2.0 * rate) * mode(m)
 
     for copy in consts[2:]:
@@ -286,42 +302,56 @@
 
     pl.loop(0, 2)(near_chunk)
 
-    pltpu.make_async_copy(
-        recv1.at[pl.ds(0, 3 * (CTX - 1))], recv1.at[pl.ds(0, 3 * (CTX - 1))], r1
-    ).wait()
     idx_copy.wait()
-    parts = [recv1[3 * i] for i in range(4)]
-    for i in range(4, CTX):
-        parts[i % 4] = parts[i % 4] + recv1[3 * i]
-    state = (parts[0] + parts[1]) + (parts[2] + parts[3])
-    a = dec2s[me]
-    aa = a * a
-    for j in range(CTX):
-        first, second = [recv1[idx_s[0, 2 * j + q]] for q in range(2)]
-        incoming[2 * j] = state
-        incoming[2 * j + 1] = a * state + first
-        state = aa * state + (a * first + second)
-    for s in range(2 * CTX):
-        send2[s // 2, s % 2] = incoming[order[s]]
-
-    for to in peers:
-        pltpu.make_async_remote_copy(
-            src_ref=send2.at[to], dst_ref=recv2.at[me], send_sem=s2, recv_sem=r2,
-            device_id=(to, mc), device_id_type=MESH,
-        ).start()
-
-    for q in range(2):
-        recv2[me, q] = send2[me, q]
+
+    @pl.when(serves)
+    def _():
+        first31 = recv1.at[pl.ds(0, CTX - 1)]
+        pltpu.make_async_copy(first31, first31, r1).wait()
+        for i in range(PER):
+            parts = [recv1[c, i, 0] for c in range(4)]
+            for c in range(4, CTX):
+                parts[c % 4] = parts[c % 4] + recv1[c, i, 0]
+            state = (parts[0] + parts[1]) + (parts[2] + parts[3])
+            a = dec2[number * PER + i]
+            aa = a * a
+            for j in range(CTX):
+                slots = [idx_s[0, 2 * j + q] for q in range(2)]
+                first, second = [recv1[lax.div(slot, 2), i, 1 + lax.rem(slot, 2)] for slot in slots]
+                incoming[2 * j] = state
+                incoming[2 * j + 1] = a * state + first
+                state = aa * state + (a * first + second)
+            for s in range(2 * CTX):
+                send2[s // 2, i, s % 2] = incoming[order[s]]
+        for to in BY_START:
+
+            @pl.when(me != to)
+            def _():
+                pltpu.make_async_remote_copy(
+                    src_ref=send2.at[to], dst_ref=recv2.at[pl.ds(number * PER, PER)],
+                    send_sem=s2, recv_sem=r2, device_id=(to, mc), device_id_type=MESH,
+                ).start()
+
+        for i in range(PER):
+            recv2[number * PER + i] = send2[me, i]
 
     pl.loop(2, 4)(near_chunk)
 
     gate_copy.wait()
-    pltpu.make_async_copy(recv2.at[pl.ds(0, CTX - 1)], recv2.at[pl.ds(0, CTX - 1)], r2).wait()
+    @pl.when(serves)
+    def _():
+        rest = recv2.at[pl.ds(0, MODES - PER)]
+        pltpu.make_async_copy(rest, rest, r2).wait()
+
+    @pl.when(jnp.logical_not(serves))
+    def _():
+        pltpu.make_async_copy(recv2, recv2, r2).wait()
+
 
     for m in range(MODES):
         scale = coef[m] * step1[m]
         for q in range(2):
-            state = jnp.concatenate([recv2[2 * m, q], recv2[2 * m + 1, q]], 0)
+            state = recv2[m, q]
             gm[2 * q, m] = state * scale
             gm[2 * q + 1, m] = (state * dec1[m] + mid[q, m]) * scale
 
@@ -377,8 +407,17 @@
                 cols = pl.ds(l * 128, 128)
                 out[rows, cols] = (near[rows, cols] * column * gain_v[:, cols]).astype(BF16)
 
-    pltpu.make_async_copy(send1.at[pl.ds(0, CTX - 1)], send1.at[pl.ds(0, CTX - 1)], s1).wait()
-    pltpu.make_async_copy(send2.at[pl.ds(0, CTX - 1)], send2.at[pl.ds(0, CTX - 1)], s2).wait()
+    @pl.when(jnp.logical_not(serves))
+    def _():
+        pltpu.make_async_copy(send1, send1, s1).wait()
+
+    @pl.when(serves)
+    def _():
+        rest = send1.at[pl.ds(0, MODES - PER)]
+        pltpu.make_async_copy(rest, rest, s1).wait()
+        sent = send2.at[pl.ds(0, CTX - 1)]
+        pltpu.make_async_copy(sent, sent, s2).wait()
+
     pltpu.make_async_copy(rss.at[pl.ds(0, CH - 1)], rss.at[pl.ds(0, CH - 1)], s3).wait()
 
 
@@ -410,7 +449,7 @@
         vmem((MODES, 8, 128), F32),
         vmem((MODES, 8, 128), F32),
         vmem((MODES, 8, 128), F32),
-        vmem((2 * MODES, 4, 128), F32),
+        vmem((MODES, 8, 128), F32),
         vmem((MODES, 8, 128), F32),
         vmem((2, MODES, 8, 128), F32),
         vmem((4, 2 * LEN, 256), F32),
@@ -422,11 +461,11 @@
         vmem((4, MODES, 8, 128), F32),
         vmem((4, 128, 128), F32),
         vmem((4, 3 * ORD, CHANS), BF16),
-        vmem((CTX, 3, 4, 128), F32),
-        vmem((3 * CTX, 4, 128), F32),
-        vmem((2 * CTX, 4, 128), F32),
-        vmem((CTX, 2, 4, 128), F32),
-        vmem((CTX, 2, 4, 128), F32),
+        vmem((MODES, 3, 8, 128), F32),
+        vmem((CTX, PER, 3, 8, 128), F32),
+        vmem((2 * CTX, 8, 128), F32),
+        vmem((CTX, PER, 2, 8, 128), F32),
+        vmem((MODES, 2, 8, 128), F32),
         vmem((4, LEN, 128), F32),
         vmem((4, 2, 128), F32),
         vmem((4, CH, 2, 128), F32),

time: 29.4 us -> 28 us (0.952)
  Pallas kernels: 27.3 us -> 25.9 us
    pallas_call x1, Pallas kernels: 27.3 us -> 25.9 us  [local(): pl.pallas_call(functools.partial(kernel, places), out_shape=pltpu.VMEM((4...]
where the time goes in v3:
time: 28 us; the launch traced here: 27.9 us
  Pallas kernels  25.9 us (92%)
  local copies, waits for them, and re-layouts  1.32 us (5%)
  between operations  0.66 us (2%)
    pallas_call x1, Pallas kernels, local(): pl.pallas_call(functools.partial(kernel, places), out_shape=pltpu.VMEM((4...  25.9 us
    unnamed x1, local copies, waits for them, and re-layouts  1.32 us

profile of v3, /device:TPU:1, one launch (start us, length us, event | category | flops | bytes accessed | tf_op | source)
XLA Modules:
  0.0 27.9 jit_solution(7378932410970358647)
XLA Ops:
  0.7 25.9 %shard_map.91 = bf16[1024,1024]{1,0:T(8,128)(2,1)S(1)} custom-call(s32[1]{0:T(128)S(6)} %copy.12.blocks, s32[64]{0:T(128)} %order_h.1, bf16[512,1024]{1,0:T(8,128)(2,1)} %prefix.1, bf16[1024,1024]{1,0:T(8,128)(2,1)} %suffix.1, bf16[1024,1024]{1,0:T(8,128)(2,1)} %gates.1, f32[16,1024]{1,0:T(8,128)} %rates.1, f32[16,1024]{1,0:T(8,128)} %residues.1, ...), custom_call_target="tpu_custom_call" | custom-call | flops 6000000000 | bytes 8000000 | tf_op jit(solution)/shard_map/pallas_call | solution.py:482
  26.6 1.3 %copy.11 = bf16[1024,1024]{1,0:T(8,128)(2,1)} copy(bf16[1024,1024]{1,0:T(8,128)(2,1)S(1)} %shard_map.91) | data formatting | bytes 4194304

commit v4 on v3

--- a/solution.py
+++ b/solution.py
@@ -77,8 +77,7 @@
 
 
 BY_START = sorted(range(CTX), key=lateness)
-SERVERS = BY_START[:16]
-PER = MODES // len(SERVERS)
+SERVERS = BY_START[:MODES]
 
 
 def split(a):
@@ -100,7 +99,7 @@
     idx_v, idx_s,
     relay, zrel, zd, tt, rate_m, coef, step1, dec1, dec2, pw,
     mid, spec, prod, hr, hi, hb, grel, gm, gb, hf,
-    send1, recv1, incoming, send2, recv2, acc, ss, rss,
+    send1, recv1, ends_of, incoming, send2, recv2, acc, ss, rss,
     sem_small, sem_x, sem_gate, sem_const, sem_idx,
     s1, r1, s2, r2, s3, r3,
 ):
@@ -111,6 +110,7 @@
         pltpu.make_async_copy(rates, rate_v, sem_small.at[0]),
         pltpu.make_async_copy(residues, res_v, sem_small.at[1]),
         pltpu.make_async_copy(order_h, order, sem_small.at[2]),
+        pltpu.make_async_copy(gain, gain_v, sem_small.at[3]),
     ]
     targets = [ends] * 2 + [taps] + [forward] * 2 + [inverse] * 4 + [fart]
     consts = [
@@ -119,17 +119,17 @@
         )
         for i, ((row, count, col), target) in enumerate(zip(places, targets))
     ]
-    consts.append(pltpu.make_async_copy(gain, gain_v, sem_const.at[len(consts)]))
-    for copy in small + consts[:2]:
-        copy.start()
-    xcopies = []
-    for c in range(6):
-        src = prefix if c < 2 else suffix
-        row = (c if c < 2 else c - 2) * LEN
-        xcopies.append(
-            pltpu.make_async_copy(src.at[pl.ds(row, LEN)], x.at[pl.ds(c * LEN, LEN)], sem_x.at[c])
-        )
-    for copy in xcopies:
+    xcopies = [
+        pltpu.make_async_copy(prefix, x.at[pl.ds(0, 2 * LEN)], sem_x.at[0]),
+        pltpu.make_async_copy(
+            suffix.at[pl.ds(0, 2 * LEN)], x.at[pl.ds(2 * LEN, 2 * LEN)], sem_x.at[1]
+        ),
+        pltpu.make_async_copy(
+            suffix.at[pl.ds(2 * LEN, 2 * LEN)], x.at[pl.ds(4 * LEN, 2 * LEN)], sem_x.at[2]
+        ),
+    ]
+    gate_copy = pltpu.make_async_copy(gates, gt, sem_gate)
+    for copy in small[:1] + consts[:2] + xcopies:
         copy.start()
 
     barrier = pltpu.get_barrier_semaphore()
@@ -149,13 +149,7 @@
     for to in others:
         pl.semaphore_signal(barrier, inc=1, device_id=(me, to), device_id_type=MESH)
 
-    for copy in consts[2:]:
-        copy.start()
-    gate_copy = pltpu.make_async_copy(gates, gt, sem_gate)
-    gate_copy.start()
-
-    for copy in small:
-        copy.wait()
+    small[0].wait()
 
     def spread(read):
         for g in range(2):
@@ -185,7 +179,8 @@
     for copy in consts[:2]:
         copy.wait()
     for c in range(6):
-        xcopies[c].wait()
+        if c % 2 == 0:
+            xcopies[c // 2].wait()
         for n in range(4):
             z = dot(ends[...], x[pl.ds(c * LEN, LEN), pl.ds(n * 256, 256)])
             z = z[:ORD] + z[ORD:]
@@ -213,18 +208,16 @@
             d1 = dec1[m]
             mid[0, m] = e[i][2]
             mid[1, m] = e[i][4]
-            full = [
-                (e[i][0] * d1 + e[i][1]) * pw[m],
-                e[i][2] * d1 + e[i][3],
-                e[i][4] * d1 + e[i][5],
-            ]
-            for j in range(3):
-                send1[m, j] = full[j]
+            past = (e[i][0] * d1 + e[i][1]) * pw[m]
+            high = past.astype(BF16).astype(F32)
+            send1[m, 0] = jnp.concatenate([high, past - high], 0).astype(BF16)
+            own = [e[i][2] * d1 + e[i][3], e[i][4] * d1 + e[i][5]]
+            send1[m, 1] = jnp.concatenate(own, 0).astype(BF16)
 
     pl.semaphore_wait(barrier, replies + CH - 1)
 
     for i, to in enumerate(SERVERS):
-        part = send1.at[pl.ds(i * PER, PER)]
+        part = send1.at[i]
 
         @pl.when(me != to)
         def _():
@@ -236,6 +229,11 @@
         @pl.when(me == to)
         def _():
             recv1[me] = part[...]
+
+    for copy in small[1:] + consts[2:] + [gate_copy]:
+        copy.start()
+    for copy in small[1:]:
+        copy.wait()
 
     lane = lax.broadcasted_iota(jnp.int32, (8, 128), 1)
 
@@ -308,39 +306,42 @@
     def _():
         first31 = recv1.at[pl.ds(0, CTX - 1)]
         pltpu.make_async_copy(first31, first31, r1).wait()
-        for i in range(PER):
-            parts = [recv1[c, i, 0] for c in range(4)]
-            for c in range(4, CTX):
-                parts[c % 4] = parts[c % 4] + recv1[c, i, 0]
-            state = (parts[0] + parts[1]) + (parts[2] + parts[3])
-            a = dec2[number * PER + i]
-            aa = a * a
-            for j in range(CTX):
-                slots = [idx_s[0, 2 * j + q] for q in range(2)]
-                first, second = [recv1[lax.div(slot, 2), i, 1 + lax.rem(slot, 2)] for slot in slots]
-                incoming[2 * j] = state
-                incoming[2 * j + 1] = a * state + first
-                state = aa * state + (a * first + second)
-            for s in range(2 * CTX):
-                send2[s // 2, i, s % 2] = incoming[order[s]]
+        parts = [None] * 4
+        for c in range(CTX):
+            past = recv1[c, 0].astype(F32)
+            past = past[:8] + past[8:]
+            parts[c % 4] = past if c < 4 else parts[c % 4] + past
+            left = recv1[c, 1].astype(F32)
+            ends_of[2 * c] = left[:8]
+            ends_of[2 * c + 1] = left[8:]
+        state = (parts[0] + parts[1]) + (parts[2] + parts[3])
+        a = dec2[number]
+        aa = a * a
+        for j in range(CTX):
+            first, second = [ends_of[idx_s[0, 2 * j + q]] for q in range(2)]
+            incoming[2 * j] = state
+            incoming[2 * j + 1] = a * state + first
+            state = aa * state + (a * first + second)
+        for c in range(CTX):
+            both = [incoming[order[2 * c + q]] for q in range(2)]
+            send2[c] = jnp.concatenate(both, 0).astype(BF16)
         for to in BY_START:
 
             @pl.when(me != to)
             def _():
                 pltpu.make_async_remote_copy(
-                    src_ref=send2.at[to], dst_ref=recv2.at[pl.ds(number * PER, PER)],
+                    src_ref=send2.at[to], dst_ref=recv2.at[number],
                     send_sem=s2, recv_sem=r2, device_id=(to, mc), device_id_type=MESH,
                 ).start()
 
-        for i in range(PER):
-            recv2[number * PER + i] = send2[me, i]
+        recv2[number] = send2[me]
 
     pl.loop(2, 4)(near_chunk)
 
     gate_copy.wait()
     @pl.when(serves)
     def _():
-        rest = recv2.at[pl.ds(0, MODES - PER)]
+        rest = recv2.at[pl.ds(0, MODES - 1)]
         pltpu.make_async_copy(rest, rest, r2).wait()
 
     @pl.when(jnp.logical_not(serves))
@@ -350,8 +351,9 @@
 
     for m in range(MODES):
         scale = coef[m] * step1[m]
+        both = recv2[m].astype(F32)
         for q in range(2):
-            state = recv2[m, q]
+            state = both[8 * q : 8 * q + 8]
             gm[2 * q, m] = state * scale
             gm[2 * q + 1, m] = (state * dec1[m] + mid[q, m]) * scale
 
@@ -413,7 +415,7 @@
 
     @pl.when(serves)
     def _():
-        rest = send1.at[pl.ds(0, MODES - PER)]
+        rest = send1.at[pl.ds(0, MODES - 1)]
         pltpu.make_async_copy(rest, rest, s1).wait()
         sent = send2.at[pl.ds(0, CTX - 1)]
         pltpu.make_async_copy(sent, sent, s2).wait()
@@ -461,18 +463,19 @@
         vmem((4, MODES, 8, 128), F32),
         vmem((4, 128, 128), F32),
         vmem((4, 3 * ORD, CHANS), BF16),
-        vmem((MODES, 3, 8, 128), F32),
-        vmem((CTX, PER, 3, 8, 128), F32),
+        vmem((MODES, 2, 16, 128), BF16),
+        vmem((CTX, 2, 16, 128), BF16),
         vmem((2 * CTX, 8, 128), F32),
-        vmem((CTX, PER, 2, 8, 128), F32),
-        vmem((MODES, 2, 8, 128), F32),
+        vmem((2 * CTX, 8, 128), F32),
+        vmem((CTX, 16, 128), BF16),
+        vmem((MODES, 16, 128), BF16),
         vmem((4, LEN, 128), F32),
         vmem((4, 2, 128), F32),
         vmem((4, CH, 2, 128), F32),
+        dma((4,)),
         dma((3,)),
-        dma((6,)),
         dma,
-        dma((len(places) + 1,)),
+        dma((len(places),)),
         dma,
         dma, dma, dma, dma, dma, dma((4,)),
     ]

time: 28 us -> 26.8 us (0.957)
  Pallas kernels: 25.9 us -> 24.6 us
    pallas_call x1, Pallas kernels: 25.9 us -> 24.6 us  [local(): pl.pallas_call(functools.partial(kernel, places), out_shape=pltpu.VMEM((4...]
where the time goes in v4:
time: 26.8 us; the launch traced here: 26.6 us
  Pallas kernels  24.6 us (92%)
  local copies, waits for them, and re-layouts  1.32 us (5%)
  between operations  0.66 us (2%)
    pallas_call x1, Pallas kernels, local(): pl.pallas_call(functools.partial(kernel, places), out_shape=pltpu.VMEM((4...  24.6 us
    unnamed x1, local copies, waits for them, and re-layouts  1.32 us

profile of v4, /device:TPU:1, one launch (start us, length us, event | category | flops | bytes accessed | tf_op | source)
XLA Modules:
  0.0 26.6 jit_solution(1840996086805240327)
XLA Ops:
  0.7 24.6 %shard_map.91 = bf16[1024,1024]{1,0:T(8,128)(2,1)S(1)} custom-call(s32[1]{0:T(128)S(6)} %copy.12.blocks, s32[64]{0:T(128)} %order_h.1, bf16[512,1024]{1,0:T(8,128)(2,1)} %prefix.1, bf16[1024,1024]{1,0:T(8,128)(2,1)} %suffix.1, bf16[1024,1024]{1,0:T(8,128)(2,1)} %gates.1, f32[16,1024]{1,0:T(8,128)} %rates.1, f32[16,1024]{1,0:T(8,128)} %residues.1, ...), custom_call_target="tpu_custom_call" | custom-call | flops 6000000000 | bytes 8000000 | tf_op jit(solution)/shard_map/pallas_call | solution.py:485
  25.3 1.3 %copy.11 = bf16[1024,1024]{1,0:T(8,128)(2,1)} copy(bf16[1024,1024]{1,0:T(8,128)(2,1)S(1)} %shard_map.91) | data formatting | bytes 4194304

commit v5 on v4

--- a/solution.py
+++ b/solution.py
@@ -77,7 +77,8 @@
 
 
 BY_START = sorted(range(CTX), key=lateness)
-SERVERS = BY_START[:MODES]
+SERVERS = BY_START[:8]
+PER = MODES // len(SERVERS)
 
 
 def split(a):
@@ -99,7 +100,7 @@
     idx_v, idx_s,
     relay, zrel, zd, tt, rate_m, coef, step1, dec1, dec2, pw,
     mid, spec, prod, hr, hi, hb, grel, gm, gb, hf,
-    send1, recv1, ends_of, incoming, send2, recv2, acc, ss, rss,
+    send1, recv1, incoming, send2, recv2, acc, ss, rss,
     sem_small, sem_x, sem_gate, sem_const, sem_idx,
     s1, r1, s2, r2, s3, r3,
 ):
@@ -203,16 +204,18 @@
                 t = tt[first + i, k]
                 for c in range(6):
                     e[i][c] = t * z[c] if k == 0 else e[i][c] + t * z[c]
-        for i in range(4):
-            m = first + i
-            d1 = dec1[m]
-            mid[0, m] = e[i][2]
-            mid[1, m] = e[i][4]
-            past = (e[i][0] * d1 + e[i][1]) * pw[m]
-            high = past.astype(BF16).astype(F32)
-            send1[m, 0] = jnp.concatenate([high, past - high], 0).astype(BF16)
-            own = [e[i][2] * d1 + e[i][3], e[i][4] * d1 + e[i][5]]
-            send1[m, 1] = jnp.concatenate(own, 0).astype(BF16)
+        for j in range(2):
+            states = [[], [], []]
+            for i in (2 * j, 2 * j + 1):
+                m = first + i
+                d1 = dec1[m]
+                mid[0, m] = e[i][2]
+                mid[1, m] = e[i][4]
+                states[0].append((e[i][0] * d1 + e[i][1]) * pw[m])
+                states[1].append(e[i][2] * d1 + e[i][3])
+                states[2].append(e[i][4] * d1 + e[i][5])
+            for q in range(3):
+                send1[first // 2 + j, q] = jnp.concatenate(states[q], 0).astype(BF16)
 
     pl.semaphore_wait(barrier, replies + CH - 1)
 
@@ -309,22 +312,21 @@
         parts = [None] * 4
         for c in range(CTX):
             past = recv1[c, 0].astype(F32)
-            past = past[:8] + past[8:]
             parts[c % 4] = past if c < 4 else parts[c % 4] + past
-            left = recv1[c, 1].astype(F32)
-            ends_of[2 * c] = left[:8]
-            ends_of[2 * c + 1] = left[8:]
         state = (parts[0] + parts[1]) + (parts[2] + parts[3])
-        a = dec2[number]
+        a = jnp.concatenate([dec2[PER * number + i] for i in range(PER)], 0)
         aa = a * a
         for j in range(CTX):
-            first, second = [ends_of[idx_s[0, 2 * j + q]] for q in range(2)]
+            slots = [idx_s[0, 2 * j + q] for q in range(2)]
+            first, second = [
+                recv1[lax.div(slot, 2), 1 + lax.rem(slot, 2)].astype(F32) for slot in slots
+            ]
             incoming[2 * j] = state
             incoming[2 * j + 1] = a * state + first
             state = aa * state + (a * first + second)
         for c in range(CTX):
-            both = [incoming[order[2 * c + q]] for q in range(2)]
-            send2[c] = jnp.concatenate(both, 0).astype(BF16)
+            for q in range(2):
+                send2[c, q] = incoming[order[2 * c + q]].astype(BF16)
         for to in BY_START:
 
             @pl.when(me != to)
@@ -341,7 +343,7 @@
     gate_copy.wait()
     @pl.when(serves)
     def _():
-        rest = recv2.at[pl.ds(0, MODES - 1)]
+        rest = recv2.at[pl.ds(0, len(SERVERS) - 1)]
         pltpu.make_async_copy(rest, rest, r2).wait()
 
     @pl.when(jnp.logical_not(serves))
@@ -349,13 +351,15 @@
         pltpu.make_async_copy(recv2, recv2, r2).wait()
 
 
-    for m in range(MODES):
-        scale = coef[m] * step1[m]
-        both = recv2[m].astype(F32)
+    for i in range(len(SERVERS)):
         for q in range(2):
-            state = both[8 * q : 8 * q + 8]
-            gm[2 * q, m] = state * scale
-            gm[2 * q + 1, m] = (state * dec1[m] + mid[q, m]) * scale
+            both = recv2[i, q].astype(F32)
+            for j in range(PER):
+                m = PER * i + j
+                state = both[8 * j : 8 * j + 8]
+                scale = coef[m] * step1[m]
+                gm[2 * q, m] = state * scale
+                gm[2 * q + 1, m] = (state * dec1[m] + mid[q, m]) * scale
 
     @pl.loop(0, ORD, step=4)
     def _(first):
@@ -415,7 +419,7 @@
 
     @pl.when(serves)
     def _():
-        rest = send1.at[pl.ds(0, MODES - 1)]
+        rest = send1.at[pl.ds(0, len(SERVERS) - 1)]
         pltpu.make_async_copy(rest, rest, s1).wait()
         sent = send2.at[pl.ds(0, CTX - 1)]
         pltpu.make_async_copy(sent, sent, s2).wait()
@@ -463,12 +467,11 @@
         vmem((4, MODES, 8, 128), F32),
         vmem((4, 128, 128), F32),
         vmem((4, 3 * ORD, CHANS), BF16),
-        vmem((MODES, 2, 16, 128), BF16),
+        vmem((len(SERVERS), 3, 16, 128), BF16),
+        vmem((CTX, 3, 16, 128), BF16),
+        vmem((2 * CTX, 16, 128), F32),
         vmem((CTX, 2, 16, 128), BF16),
-        vmem((2 * CTX, 8, 128), F32),
-        vmem((2 * CTX, 8, 128), F32),
-        vmem((CTX, 16, 128), BF16),
-        vmem((MODES, 16, 128), BF16),
+        vmem((len(SERVERS), 2, 16, 128), BF16),
         vmem((4, LEN, 128), F32),
         vmem((4, 2, 128), F32),
         vmem((4, CH, 2, 128), F32),

time: 26.8 us -> 26.3 us (0.981)
  Pallas kernels: 24.6 us -> 24.2 us
    pallas_call x1, Pallas kernels: 24.6 us -> 24.2 us  [local(): pl.pallas_call(functools.partial(kernel, places), out_shape=pltpu.VMEM((4...]
where the time goes in v5:
time: 26.3 us; the launch traced here: 26.2 us
  Pallas kernels  24.2 us (92%)
  local copies, waits for them, and re-layouts  1.32 us (5%)
  between operations  0.66 us (3%)
    pallas_call x1, Pallas kernels, local(): pl.pallas_call(functools.partial(kernel, places), out_shape=pltpu.VMEM((4...  24.2 us
    unnamed x1, local copies, waits for them, and re-layouts  1.32 us

profile of v5, /device:TPU:1, one launch (start us, length us, event | category | flops | bytes accessed | tf_op | source)
XLA Modules:
  0.0 26.2 jit_solution(13311048337146619676)
XLA Ops:
  0.7 24.2 %shard_map.91 = bf16[1024,1024]{1,0:T(8,128)(2,1)S(1)} custom-call(s32[1]{0:T(128)S(6)} %copy.12.blocks, s32[64]{0:T(128)} %order_h.1, bf16[512,1024]{1,0:T(8,128)(2,1)} %prefix.1, bf16[1024,1024]{1,0:T(8,128)(2,1)} %suffix.1, bf16[1024,1024]{1,0:T(8,128)(2,1)} %gates.1, f32[16,1024]{1,0:T(8,128)} %rates.1, f32[16,1024]{1,0:T(8,128)} %residues.1, ...), custom_call_target="tpu_custom_call" | custom-call | flops 6000000000 | bytes 8000000 | tf_op jit(solution)/shard_map/pallas_call | solution.py:488
  24.8 1.3 %copy.11 = bf16[1024,1024]{1,0:T(8,128)(2,1)} copy(bf16[1024,1024]{1,0:T(8,128)(2,1)S(1)} %shard_map.91) | data formatting | bytes 4194304

commit v6 on v5

--- a/solution.py
+++ b/solution.py
@@ -77,7 +77,7 @@
 
 
 BY_START = sorted(range(CTX), key=lateness)
-SERVERS = BY_START[:8]
+SERVERS = [0, 1, 4, 16, 2, 8, 3, 20]
 PER = MODES // len(SERVERS)
 
 
@@ -190,8 +190,6 @@
                     zrel[c, pl.ds(g * 64 + (2 * n + h) * 8, 8), :] = z[
                         g * 8 : g * 8 + 8, h * 128 : h * 128 + 128
                     ]
-
-    for c in range(6):
         for k in range(ORD):
             zd[c, k] = zrel[c, pl.ds(k // 8 * 64 + k % 8, 8, stride=8), :]
 
@@ -394,17 +392,18 @@
         sums = sums + lax.dot_general(ones, low, dims, preferred_element_type=F32)
         ss[c, pl.ds(0, 1), :] = sums[:1, :128]
         ss[c, pl.ds(1, 1), :] = sums[:1, 128:]
-        for to in others:
+        rss[c // 2, mc, c % 2] = ss[c]
+        for to in others if c % 2 else []:
             pltpu.make_async_remote_copy(
-                src_ref=ss.at[c], dst_ref=rss.at[c, mc], send_sem=s3, recv_sem=r3.at[c],
+                src_ref=ss.at[pl.ds(c - 1, 2)], dst_ref=rss.at[c // 2, mc], send_sem=s3, recv_sem=r3.at[c],
                 device_id=(me, to), device_id_type=MESH,
             ).start()
-        rss[c, mc] = ss[c]
 
     for c in range(4):
-        three = rss.at[c, pl.ds(0, CH - 1)]
-        pltpu.make_async_copy(three, three, r3.at[c]).wait()
-        total = (rss[c, 0] + rss[c, 1]) + (rss[c, 2] + rss[c, 3])
+        if c % 2 == 0:
+            three = rss.at[c // 2, pl.ds(0, CH - 1)]
+            pltpu.make_async_copy(three, three, r3.at[c + 1]).wait()
+        total = (rss[c // 2, 0, c % 2] + rss[c // 2, 1, c % 2]) + (rss[c // 2, 2, c % 2] + rss[c // 2, 3, c % 2])
         factor = lax.rsqrt(total * (1.0 / (CH * CHANS)) + EPS)
         for g in range(2):
             rows = pl.ds(c * LEN + g * 128, 128)
@@ -424,7 +423,8 @@
         sent = send2.at[pl.ds(0, CTX - 1)]
         pltpu.make_async_copy(sent, sent, s2).wait()
 
-    pltpu.make_async_copy(rss.at[pl.ds(0, CH - 1)], rss.at[pl.ds(0, CH - 1)], s3).wait()
+    sent = rss.at[:, pl.ds(0, CH - 1)]
+    pltpu.make_async_copy(sent, sent, s3).wait()
 
 
 def local(prefix, suffix, gates, rates, residues, gain, order, blocks):
@@ -474,7 +474,7 @@
         vmem((len(SERVERS), 2, 16, 128), BF16),
         vmem((4, LEN, 128), F32),
         vmem((4, 2, 128), F32),
-        vmem((4, CH, 2, 128), F32),
+        vmem((2, CH, 2, 2, 128), F32),
         dma((4,)),
         dma((3,)),
         dma,

time: 26.3 us -> 25.9 us (0.985)
  Pallas kernels: 24.2 us -> 23.8 us
    pallas_call x1, Pallas kernels: 24.2 us -> 23.8 us  [local(): pl.pallas_call(functools.partial(kernel, places), out_shape=pltpu.VMEM((4...]
where the time goes in v6:
time: 25.9 us; the launch traced here: 25.7 us
  Pallas kernels  23.8 us (92%)
  local copies, waits for them, and re-layouts  1.32 us (5%)
  between operations  0.66 us (3%)
    pallas_call x1, Pallas kernels, local(): pl.pallas_call(functools.partial(kernel, places), out_shape=pltpu.VMEM((4...  23.8 us
    unnamed x1, local copies, waits for them, and re-layouts  1.32 us

profile of v6, /device:TPU:1, one launch (start us, length us, event | category | flops | bytes accessed | tf_op | source)
XLA Modules:
  0.0 25.7 jit_solution(4048568515793523317)
XLA Ops:
  0.7 23.8 %shard_map.91 = bf16[1024,1024]{1,0:T(8,128)(2,1)S(1)} custom-call(s32[1]{0:T(128)S(6)} %copy.12.blocks, s32[64]{0:T(128)} %order_h.1, bf16[512,1024]{1,0:T(8,128)(2,1)} %prefix.1, bf16[1024,1024]{1,0:T(8,128)(2,1)} %suffix.1, bf16[1024,1024]{1,0:T(8,128)(2,1)} %gates.1, f32[16,1024]{1,0:T(8,128)} %rates.1, f32[16,1024]{1,0:T(8,128)} %residues.1, ...), custom_call_target="tpu_custom_call" | custom-call | flops 6000000000 | bytes 8000000 | tf_op jit(solution)/shard_map/pallas_call | solution.py:488
  24.4 1.3 %copy.11 = bf16[1024,1024]{1,0:T(8,128)(2,1)} copy(bf16[1024,1024]{1,0:T(8,128)(2,1)S(1)} %shard_map.91) | data formatting | bytes 4194304

commit v7 on v6

--- a/solution.py
+++ b/solution.py
@@ -375,7 +375,7 @@
     for c in range(4):
         natural(gb.at[c], hf.at[c])
 
-    ones = jnp.ones((8, 128), BF16)
+    ones = jnp.ones((8, 256), BF16)
     for c in range(4):
         rows = pl.ds(c * LEN, LEN)
         for n in range(4):
@@ -388,8 +388,8 @@
             acc[c] = square if n == 0 else acc[c] + square
         high, low = split(acc[c])
         dims = (((1,), (1,)), ((), ()))
-        sums = lax.dot_general(ones, high, dims, preferred_element_type=F32)
-        sums = sums + lax.dot_general(ones, low, dims, preferred_element_type=F32)
+        halved = jnp.concatenate([high, low], 1)
+        sums = lax.dot_general(ones, halved, dims, preferred_element_type=F32)
         ss[c, pl.ds(0, 1), :] = sums[:1, :128]
         ss[c, pl.ds(1, 1), :] = sums[:1, 128:]
         rss[c // 2, mc, c % 2] = ss[c]

time: 25.9 us -> 25.8 us (level)
  no operation moved by 1% of the time
where the time goes in v7:
time: 25.8 us; the launch traced here: 25.6 us
  Pallas kernels  23.7 us (92%)
  local copies, waits for them, and re-layouts  1.32 us (5%)
  between operations  0.66 us (3%)
    pallas_call x1, Pallas kernels, local(): pl.pallas_call(functools.partial(kernel, places), out_shape=pltpu.VMEM((4...  23.7 us
    unnamed x1, local copies, waits for them, and re-layouts  1.32 us

profile of v7, /device:TPU:1, one launch (start us, length us, event | category | flops | bytes accessed | tf_op | source)
XLA Modules:
  0.0 25.6 jit_solution(12053827922018711502)
XLA Ops:
  0.7 23.7 %shard_map.91 = bf16[1024,1024]{1,0:T(8,128)(2,1)S(1)} custom-call(s32[1]{0:T(128)S(6)} %copy.12.blocks, s32[64]{0:T(128)} %order_h.1, bf16[512,1024]{1,0:T(8,128)(2,1)} %prefix.1, bf16[1024,1024]{1,0:T(8,128)(2,1)} %suffix.1, bf16[1024,1024]{1,0:T(8,128)(2,1)} %gates.1, f32[16,1024]{1,0:T(8,128)} %rates.1, f32[16,1024]{1,0:T(8,128)} %residues.1, ...), custom_call_target="tpu_custom_call" | custom-call | flops 6000000000 | bytes 8000000 | tf_op jit(solution)/shard_map/pallas_call | solution.py:488
  24.3 1.3 %copy.11 = bf16[1024,1024]{1,0:T(8,128)(2,1)} copy(bf16[1024,1024]{1,0:T(8,128)(2,1)S(1)} %shard_map.91) | data formatting | bytes 4194304

commit v8 on v7

--- a/solution.py
+++ b/solution.py
@@ -382,7 +382,7 @@
             cols = pl.ds(n * 256, 256)
             value = near[rows, cols] + dot(fart[:, : 3 * ORD], hf[c, :, cols])
             value = value * gt[rows, cols].astype(F32)
-            near[rows, cols] = value
+            near[rows, cols] = value * gain_v[:, cols]
             square = value * value
             square = square[:, :128] + square[:, 128:]
             acc[c] = square if n == 0 else acc[c] + square
@@ -410,7 +410,7 @@
             column = jnp.transpose(jnp.broadcast_to(factor[g : g + 1, :], (128, 128)))
             for l in range(TILES):
                 cols = pl.ds(l * 128, 128)
-                out[rows, cols] = (near[rows, cols] * column * gain_v[:, cols]).astype(BF16)
+                out[rows, cols] = (near[rows, cols] * column).astype(BF16)
 
     @pl.when(jnp.logical_not(serves))
     def _():

time: 25.8 us -> 25.9 us (level)
  no operation moved by 1% of the time
where the time goes in v8:
time: 25.9 us; the launch traced here: 25.7 us
  Pallas kernels  23.8 us (92%)
  local copies, waits for them, and re-layouts  1.32 us (5%)
  between operations  0.66 us (3%)
    pallas_call x1, Pallas kernels, local(): pl.pallas_call(functools.partial(kernel, places), out_shape=pltpu.VMEM((4...  23.8 us
    unnamed x1, local copies, waits for them, and re-layouts  1.32 us

profile of v8, /device:TPU:1, one launch (start us, length us, event | category | flops | bytes accessed | tf_op | source)
XLA Modules:
  0.0 25.7 jit_solution(5828549463504233362)
XLA Ops:
  0.7 23.8 %shard_map.91 = bf16[1024,1024]{1,0:T(8,128)(2,1)S(1)} custom-call(s32[1]{0:T(128)S(6)} %copy.12.blocks, s32[64]{0:T(128)} %order_h.1, bf16[512,1024]{1,0:T(8,128)(2,1)} %prefix.1, bf16[1024,1024]{1,0:T(8,128)(2,1)} %suffix.1, bf16[1024,1024]{1,0:T(8,128)(2,1)} %gates.1, f32[16,1024]{1,0:T(8,128)} %rates.1, f32[16,1024]{1,0:T(8,128)} %residues.1, ...), custom_call_target="tpu_custom_call" | custom-call | flops 6000000000 | bytes 8000000 | tf_op jit(solution)/shard_map/pallas_call | solution.py:488
  24.4 1.3 %copy.11 = bf16[1024,1024]{1,0:T(8,128)(2,1)} copy(bf16[1024,1024]{1,0:T(8,128)(2,1)S(1)} %shard_map.91) | data formatting | bytes 4194304
